TPU v7x, 256 devices: a whole 4x4x8 slice. The times are simulated.
256 devices in a mesh: samp: 16 (over z, x_lo), tok: 16 (over x_hi, y, core).
Axes of the slice: x: 4 (x_hi: 2, x_lo: 2; x = x_hi * 2 + x_lo), y: 4, z: 8, core: 2. Of those that a mesh axis runs over, the one named last changes fastest.
Arguments:
- features_in: bfloat16 [16, 256, 512, 128], P('samp', 'tok'), may hold values from -6 to 6
- path_noise: bfloat16 [16, 256, 512, 128], P('samp', 'tok'), may hold values from -6 to 6
- latent: float32 [16, 512], P('samp'), may hold values from -6 to 6
- bank: bfloat16 [8, 9, 128, 128], replicated, may hold values from -0.1875 to 0.1875
- style_weight: float32 [512, 128], replicated, may hold values from -0.25 to 0.25
- select_weight: float32 [512, 8], replicated, may hold values from -0.25 to 0.25
- path_mean: float32 [1], replicated, may hold values from 0.5 to 2
Outputs:
- features: bfloat16 [16, 256, 512, 128], P('samp', 'tok')
- penalty: float32 [16], P('samp')
- bank_grad: float32 [8, 9, 128, 128], P(None, None, 'samp')
- style_grad: float32 [512, 128], replicated
- select_grad: float32 [512, 8], replicated
All inputs are finite; a program needn't handle non-finite values.
Results may differ from a plain program's by a relative error of at most 0.0049.
Values may be sent and summed in bfloat16 or wider, within the bound.
No kernel may reach another device: no remote copies, remote signals or barrier semaphores. Data moves between devices by JAX's collectives and lax.ppermute only.
A program may use at most 128 MiB of HBM per device.

v0:
```python
import math

import jax
import jax.numpy as jnp
from jax import lax
from jax.sharding import PartitionSpec as P

HIGH = lax.Precision.HIGHEST


def with_halo(block, sides, width):
    for axis, dim in sides:
        count = lax.axis_size(axis)
        forward = [(i, i + 1) for i in range(count - 1)]
        backward = [(target, source) for source, target in forward]
        low = lax.ppermute(
            lax.slice_in_dim(block, block.shape[dim] - width, None, axis=dim), axis, forward
        )
        high = lax.ppermute(lax.slice_in_dim(block, 0, width, axis=dim), axis, backward)
        block = jnp.concatenate([low, block, high], axis=dim)
    return block


def mixing(wvec, select_w):
    logits = jnp.dot(wvec, select_w, precision=HIGH)
    expo = jnp.exp(logits)
    return expo / jnp.sum(expo)


def modulate(wvec, kern, style_w):
    style = jnp.dot(wvec, style_w, precision=HIGH) + 1.0
    scaled = kern * style[None, :, None]
    demod = lax.rsqrt(jnp.sum(scaled * scaled, axis=(0, 1)) + 1e-08)
    return scaled * demod[None, None, :]


def kernel_of(wvec, bank32, style_w, select_w):
    mixed = jnp.einsum("b,bkio->kio", mixing(wvec, select_w), bank32, precision=HIGH)
    return modulate(wvec, mixed, style_w)


def path_grad(wvec, corr_one, bank32, style_w, select_w):
    return jax.grad(lambda v: jnp.sum(corr_one * kernel_of(v, bank32, style_w, select_w)))(wvec)


def penalty_of(wvec, corr_one, bank32, style_w, select_w, target):
    grad_w = path_grad(wvec, corr_one, bank32, style_w, select_w)
    length = jnp.sqrt(jnp.sum(grad_w * grad_w) + 1e-08)
    return (length - target) ** 2


def local(features_in, path_noise, latent, bank, style_weight, select_weight, path_mean):
    count, rows, cols, chans = features_in.shape
    images = count * lax.axis_size("samp")
    height = rows * lax.axis_size("tok")
    padded_rows = with_halo(features_in, (("tok", 1),), 1)
    padded = jnp.pad(padded_rows, ((0, 0), (0, 0), (1, 1), (0, 0)))
    bank32 = bank.astype(jnp.float32)
    kernels = jax.vmap(kernel_of, (0, None, None, None))(
        latent, bank32, style_weight, select_weight
    )
    kernel_low = kernels.astype(jnp.bfloat16)
    total = jnp.zeros((count, rows, cols, chans), jnp.float32)
    corr_taps = []
    for tap in range(9):
        ky, kx = (tap // 3, tap % 3)
        window = padded[:, ky : ky + rows, kx : kx + cols, :]
        total = total + jnp.einsum(
            "nrci,nio->nrco", window, kernel_low[:, tap], preferred_element_type=jnp.float32
        )
        corr_taps.append(
            jnp.einsum("nrci,nrco->nio", window, path_noise, preferred_element_type=jnp.float32)
        )
    features = total.astype(jnp.bfloat16)
    corr_local = jnp.stack(corr_taps, 1)
    corr = lax.psum(corr_local, "tok") * (1.0 / math.sqrt(height * cols))
    target = path_mean[0]
    weights = jnp.full((count,), 1.0 / images, jnp.float32)

    def pens_fn(bank_f, style_w, select_w):
        return jax.vmap(penalty_of, (0, 0, None, None, None, None))(
            latent, corr, bank_f, style_w, select_w, target
        )

    pens, back = jax.vjp(pens_fn, bank32, style_weight, select_weight)
    bank_part, style_part, select_part = back(weights)
    bank_grad = lax.psum_scatter(bank_part, "samp", scatter_dimension=2, tiled=True)
    style_grad, select_grad = lax.psum((style_part, select_part), "samp")
    return (features, pens, bank_grad, style_grad, select_grad)


def solution(mesh):
    placed = (
        P("samp", "tok", None, None),
        P("samp", "tok", None, None),
        P("samp", None),
        P(),
        P(),
        P(),
        P(),
    )
    return jax.shard_map(
        local,
        mesh=mesh,
        in_specs=placed,
        out_specs=(P("samp", "tok", None, None), P("samp"), P(None, None, "samp", None), P(), P()),
        check_vma=False,
    )
```

profile of v0, /device:TPU:1, one launch (start us, length us, event | category | flops | bytes accessed | tf_op | source)
XLA Modules:
  0.0 467.3 jit_solution(189163393301264175)
XLA Ops:
  7.2 1.1 fusion.148
  8.4 4.6 collective-permute-start
  13.0 1.9 collective-permute-start.1
  15.5 1.6 fusion.149
  18.4 1.2 fusion.128
  19.7 2.8 fusion.10
  22.6 0.8 fusion.58
  23.3 1.7 copy-done.3
  25.0 0.8 fusion.66
  25.8 0.8 fusion.74
  26.6 0.8 fusion.80
  27.4 0.8 fusion.88
  28.1 0.8 fusion.96
  28.9 0.8 fusion.102
  29.7 0.8 fusion.110
  30.5 0.8 fusion.118
  31.3 0.8 copy-done.12
  33.1 2.8 fusion.47
  36.1 141.0 %all-reduce.4.cloned.1.call-done = f32[1,9,128,128]{3,2,1,0:T(8,128)} async-done(((f32[1,9,128,128]{3,2,1,0:T(8,128)}), f32[1,9,128,128]{3,2,1,0:T(8,128)}) %all-reduce.4.cloned.1.call-update) | async-done | bytes 589840 | tf_op jit(solution)/shard_map/psum | solution.py:76
  177.1 1.3 fusion.130
  179.0 1.3 broadcast_multiply_fusion
  180.3 0.8 copy-done.8
  181.1 7.3 %multiply_reduce_fusion.9 = (f32[]{:T(128)}, f32[8]{0:T(128)}) fusion(f32[8]{0:T(128)} %copy-done.26, f32[]{:T(128)} %bitcast.70, f32[9,128,128,1]{2,3,1,0:T(1,128)S(1)} %bitcast.363, bf16[8,9,128,128]{3,2,1,0:T(8,128)(2,1)S(1)} %copy-done), kind=kOutput, calls=%fused_computation.137 | convolution fusion | flops 14155799 | bytes 2949192 | tf_op jit(solution)/shard_map/jvp(vmap(transpose(jvp(b,bkio->kio))))/dot_general | solution.py:38
  189.1 1.3 fusion.146
  191.1 1.3 fusion.139
  194.3 0.7 add_multiply_fusion
  195.0 1.8 convolution_bitcast_fusion
  196.8 1.9 multiply_reduce_fusion.10
  199.3 1.3 divide_add_fusion.1
  200.6 2.8 fusion.43
  203.5 1.7 multiply_reduce_fusion
  205.2 1.0 fusion.129
  207.1 0.9 bitcast_add_fusion.2
  208.1 3.4 multiply_add_fusion
  213.6 6.2 %multiply_reduce_fusion.7 = (f32[]{:T(128)}, f32[]{:T(128)}, f32[]{:T(128)}, f32[8]{0:T(128)S(1)}) fusion(f32[8]{0:T(128)S(1)} %copy-done.39, f32[8]{0:T(128)S(1)} %copy-done.27, f32[]{:T(128)S(6)} %neg.23, f32[]{:T(128)S(6)} %div.81, f32[8]{0:T(128)S(1)} %copy-done.36, f32[9,128,128,1]{2,3,1,0:T(1,128)S(1)} %bitcast.366, ...), kind=kOutput, calls=%fused_computation.133 | convolution fusion | flops 14155853 | bytes 2949268 | tf_op jit(solution)/shard_map/transpose(jvp(vmap(jvp(b,bkio->kio))))/dot_general | solution.py:38
  222.5 50.7 %psum.23 = f32[512,8]{0,1:T(8,128)} all-reduce(f32[512,8]{0,1:T(8,128)S(1)} %bitcast_add_fusion.3), channel_id=1, replica_groups=mesh['samp'=16,'tok'=16] {'samp'}, use_global_device_ids=true, to_apply=%region_17.18 | all-reduce | flops 4096 | bytes 32768 | tf_op jit(solution)/shard_map/psum | solution.py:88
  273.2 2.4 fusion.53
  275.6 2.7 fusion.50
  278.3 2.7 fusion.39
  281.0 2.6 fusion.38
  283.7 2.7 fusion.33
  286.3 2.7 fusion.37
  289.1 2.7 fusion.36
  291.8 2.7 fusion.35
  294.5 11.8 %fusion.11 = bf16[1,16,512,128]{3,2,1,0:T(8,128)(2,1)} fusion(f32[16,512,128]{2,1,0:T(8,128)S(1)} %fusion.53, f32[16,512,128]{2,1,0:T(8,128)} %fusion.39, f32[16,512,128]{2,1,0:T(8,128)} %fusion.38, f32[128,16,512]{0,2,1:T(8,128)} %fusion.33, f32[16,512,128]{2,1,0:T(8,128)} %fusion.37, f32[16,512,128]{2,1,0:T(8,128)} %fusion.36, ...), kind=kOutput, calls=%fused_computation.15 | convolution fusion | flops 277872640 | bytes 37781504 | tf_op jit(solution)/shard_map/nrci,nio->nrco/dot_general | solution.py:68
  306.3 31.0 %all-reduce.6.cloned.1.call-done = f32[512,128]{1,0:T(8,128)} async-done(((f32[512,128]{1,0:T(8,128)}), f32[512,128]{1,0:T(8,128)}) %all-reduce.6.cloned.1.call-update) | async-done | bytes 262160 | tf_op jit(solution)/shard_map/psum | solution.py:88
  337.3 120.7 %reduce-scatter.2.cloned.1.call-done = f32[8,9,8,128]{3,2,1,0:T(8,128)} async-done(((f32[8,9,128,128]{3,2,1,0:T(8,128)}), f32[8,9,8,128]{3,2,1,0:T(8,128)}) %reduce-scatter.2.cloned.1.call-update) | async-done | bytes 294928 | tf_op jit(solution)/shard_map/reduce_scatter | solution.py:87
  458.0 1.7 copy.71
  (99 shorter events, 5.4 us)
Async XLA Ops:
  7.2 25.9 %copy-start = (bf16[8,9,128,128]{3,2,1,0:T(8,128)(2,1)S(1)}, bf16[8,9,128,128]{3,2,1,0:T(8,128)(2,1)}, u32[]{:S(2)}) copy-start(bf16[8,9,128,128]{3,2,1,0:T(8,128)(2,1)} %param.10) | copy-start | bytes 7077892
  7.2 169.9 %all-reduce.4.cloned.1.call-start = ((), (), s32[]{:S(2)}) async-start(), calls=%async_computation.1 | async-start | bytes 1179648 | tf_op jit(solution)/shard_map/psum | solution.py:76
  8.4 11.3 %collective-permute-start = (bf16[1,1,512,128]{3,2,1,0:T(8,128)(2,1)S(1)}, bf16[1,1,512,128]{3,2,1,0:T(8,128)(2,1)S(1)}, u32[]{:S(2)}, u32[]{:S(2)}) collective-permute-start(bf16[1,1,512,128]{3,2,1,0:T(8,128)(2,1)S(1)} %get-tuple-element.15), channel_id=1, source_target_pairs={{0,1},{1,2},{2,3},{3,4},{4,5},{5,6},{6,7},{7,8},{8,9},{9,10},{10,1... | collective-permute-start | bytes 393224 | tf_op jit(solution)/shard_map/ppermute | solution.py:16
  13.0 6.7 %collective-permute-start.1 = (bf16[1,1,512,128]{3,2,1,0:T(8,128)(2,1)S(1)}, bf16[1,1,512,128]{3,2,1,0:T(8,128)(2,1)S(1)}, u32[]{:S(2)}, u32[]{:S(2)}) collective-permute-start(bf16[1,1,512,128]{3,2,1,0:T(8,128)(2,1)S(1)} %get-tuple-element.16), channel_id=1, source_target_pairs={{1,0},{2,1},{3,2},{4,3},{5,4},{6,5},{7,6},{8,7},{9,8},{10,9},{11,1... | collective-permute-start | bytes 393224 | tf_op jit(solution)/shard_map/ppermute | solution.py:19
  17.1 15.3 %copy-start.26 = (f32[8]{0:T(128)}, f32[8]{0:T(128)S(1)}, u32[]{:S(2)}) copy-start(f32[8]{0:T(128)S(1)} %get-tuple-element.26) | copy-start | bytes 100
  19.6 159.3 %copy-start.20 = (f32[128]{0:T(128)}, f32[128]{0:T(128)S(1)}, u32[]{:S(2)}) copy-start(f32[128]{0:T(128)S(1)} %fusion.128) | copy-start | bytes 1540
  19.6 2.9 copy-start.10
  19.7 3.7 copy-start.13
  19.7 10.0 %copy-start.15 = (bf16[1,1,512,128]{3,2,1,0:T(8,128)(2,1)}, bf16[1,1,512,128]{3,2,1,0:T(8,128)(2,1)S(1)}, u32[]{:S(2)}) copy-start(bf16[1,1,512,128]{3,2,1,0:T(8,128)(2,1)S(1)} %collective-permute-done.1) | copy-start | bytes 393220
  22.5 8.0 %copy-start.1 = (bf16[1,18,514,128]{3,2,1,0:T(8,128)(2,1)}, bf16[1,18,514,128]{3,2,1,0:T(8,128)(2,1)S(1)}, u32[]{:S(2)}) copy-start(bf16[1,18,514,128]{3,2,1,0:T(8,128)(2,1)S(1)} %fusion.10) | copy-start | bytes 7105540
  22.5 2.5 copy-start.3
  31.3 0.8 copy-start.12
  32.2 305.1 %all-reduce.6.cloned.1.call-start = ((), (), s32[]{:S(2)}) async-start(), calls=%async_computation.3 | async-start | bytes 524288 | tf_op jit(solution)/shard_map/psum | solution.py:88
  33.1 2.8 copy-start.37
  36.1 142.9 %copy-start.30 = (f32[128]{0:T(128)}, f32[128]{0:T(128)S(1)}, u32[]{:S(2)}) copy-start(f32[128]{0:T(128)S(1)} %multiply_reduce_fusion.4) | copy-start | bytes 1540
  178.4 0.6 copy-start.32
  180.3 0.8 copy-start.8
  180.3 10.8 %copy-start.6 = (f32[1,9,128,128]{3,2,1,0:T(8,128)}, f32[1,9,128,128]{3,2,1,0:T(8,128)S(1)}, u32[]{:S(2)}) copy-start(f32[1,9,128,128]{3,2,1,0:T(8,128)S(1)} %get-tuple-element.14) | copy-start | bytes 1769476
  180.3 10.1 %copy-start.17 = (f32[512,8]{0,1:T(8,128)S(1)}, f32[512,8]{0,1:T(8,128)}, u32[]{:S(2)}) copy-start(f32[512,8]{0,1:T(8,128)} %param.12) | copy-start | bytes 49156
  190.4 0.5 copy-start.34
  190.5 1.8 copy-start.24
  191.1 1.3 copy-start.28
  192.4 0.6 copy-start.23
  195.0 3.7 copy-start.18
  195.0 10.2 %copy-start.5 = (f32[1,9,128,128]{3,2,1,0:T(8,128)S(1)}, f32[1,9,128,128]{3,2,1,0:T(8,128)}, u32[]{:S(2)}) copy-start(f32[1,9,128,128]{3,2,1,0:T(8,128)} %all-reduce.4.cloned.1.call-done) | copy-start | bytes 1769476
  198.7 4.8 %copy-start.25 = (f32[128]{0:T(128)S(1)}, f32[128]{0:T(128)}, u32[]{:S(2)}) copy-start(f32[128]{0:T(128)} %convolution_bitcast_fusion) | copy-start | bytes 1540
  203.4 2.7 copy-start.31
  203.4 2.7 copy-start.33
  203.4 2.7 copy-start.40
  203.4 2.7 copy-start.21
  203.4 2.7 copy-start.38
  205.1 1.5 copy-start.7
  206.2 0.8 copy-start.19
  206.2 0.8 copy-start.22
  206.2 0.8 copy-start.29
  206.6 1.4 copy-start.9
  208.0 250.0 %reduce-scatter.2.cloned.1.call-start = ((), (), s32[]{:S(2)}) async-start(), calls=%async_computation.2 | async-start | bytes 5013504 | tf_op jit(solution)/shard_map/reduce_scatter | solution.py:87
  211.5 2.1 copy-start.27
  211.5 2.1 copy-start.36
  211.5 2.1 copy-start.39
  211.5 10.9 %copy-start.35 = (f32[8]{0:T(128)S(1)}, f32[8]{0:T(128)}, u32[]{:S(2)}) copy-start(f32[8]{0:T(128)} %copy-done.34) | copy-start | bytes 100
  211.5 61.6 %copy-start.11 = (bf16[1,9,128,128]{3,2,1,0:T(8,128)(2,1)S(1)}, bf16[1,9,128,128]{3,2,1,0:T(8,128)(2,1)}, u32[]{:S(2)}) copy-start(bf16[1,9,128,128]{3,2,1,0:T(8,128)(2,1)} %get-tuple-element.18) | copy-start | bytes 884740
  211.5 61.6 %copy-start.16 = (bf16[1,1,512,128]{3,2,1,0:T(8,128)(2,1)S(1)}, bf16[1,1,512,128]{3,2,1,0:T(8,128)(2,1)}, u32[]{:S(2)}) copy-start(bf16[1,1,512,128]{3,2,1,0:T(8,128)(2,1)} %copy-done.15) | copy-start | bytes 393220
  273.2 2.4 copy-start.4
  273.2 2.4 copy-start.14
  275.6 2.7 copy-start.2
Sparse Core Ops, SparseCore 0:
  32.3 144.7 all-reduce.3
  208.1 129.1 all-reduce.5
  340.4 117.4 reduce-scatter.1
where the time goes:
time: 470 us; the launch traced here: 467 us
  waiting for transfers between devices  293 us (62%)
  matrix products  67.1 us (14%)
  blocking collectives  50.7 us (11%)
  between operations  23.4 us (5%)
  other arithmetic  19.4 us (4%)
  local copies, waits for them, and re-layouts  7.23 us (2%)
  starting transfers between devices  6.82 us (1%)
    psum x1, waiting for transfers between devices, local(): corr = lax.psum(corr_local, 'tok') * (1.0 / math.sqrt(height * cols))  141 us
    reduce_scatter x1, waiting for transfers between devices, local(): lax.psum_scatter(bank_part, 'samp', scatter_dimension=2, tiled=True)  121 us
    psum x1, blocking collectives, local(): style_grad, select_grad = lax.psum((style_part, select_part), 'samp')  50.7 us
    dot_general x9, matrix products, local(): jnp.einsum('nrci,nio->nrco', window, kernel_low[:, tap], preferred_elemen...  33.1 us
    psum x1, waiting for transfers between devices, local(): style_grad, select_grad = lax.psum((style_part, select_part), 'samp')  31 us
    dot_general x4, matrix products, kernel_of(): jnp.einsum('b,bkio->kio', mixing(wvec, select_w), bank32, precision=HIGH)  19.1 us
  transfers between devices with their start and end apart: 5, of which 3 were waited for; matrix products, arithmetic and copies ran while one was open for 11% of the time, Pallas kernels for 0%

commit v1 on v0

v1 whole, which is shorter than its diff:
```python
import math

import jax
import jax.numpy as jnp
from jax import lax
from jax.experimental import pallas as pl
from jax.experimental.pallas import tpu as pltpu
from jax.sharding import PartitionSpec as P

HIGH = lax.Precision.HIGHEST
EPS = 1e-08
F32 = jnp.float32
BF16 = jnp.bfloat16
TAPS = 9
C = 128
NB = 8
GROUP = 4
MIB = 1024 * 1024


def whole(count):
    return [pl.BlockSpec(memory_space=pltpu.VMEM)] * count


def call(kernel, outs, inputs, scratch=(), limit=24, flops=0, name=None):
    size = sum(math.prod(x.shape) * x.dtype.itemsize for x in inputs)
    shapes = [jax.ShapeDtypeStruct(s, d) for s, d in outs]
    return pl.pallas_call(
        kernel,
        out_shape=shapes,
        in_specs=whole(len(inputs)),
        out_specs=whole(len(outs)),
        scratch_shapes=list(scratch),
        compiler_params=pltpu.CompilerParams(vmem_limit_bytes=limit * MIB),
        cost_estimate=pl.CostEstimate(flops=flops, bytes_accessed=size, transcendentals=0),
        name=name,
    )(*inputs)


def row_dot(row, mat):
    rows = jnp.broadcast_to(row, (8, row.shape[1]))
    return jnp.dot(rows, mat, precision=HIGH, preferred_element_type=F32)[:1]


def row_dot_t(row, mat):
    rows = jnp.broadcast_to(row, (8, row.shape[1]))
    return lax.dot_general(
        rows, mat, (((1,), (1,)), ((), ())), precision=HIGH, preferred_element_type=F32
    )[:1]


def down(row):
    return jnp.broadcast_to(row, (C, C)).T


def across(col):
    size = col.shape[0]
    lane = lax.broadcasted_iota(jnp.int32, (size, C), 1)
    line = lax.broadcasted_iota(jnp.int32, (size, C), 0)
    return jnp.sum(jnp.where(lane == line, col, 0.0), axis=0, keepdims=True)


def widen(row):
    return jnp.concatenate([row, jnp.zeros((1, C - row.shape[1]), F32)], axis=1)


def weighted(bank, weights, tap):
    total = weights[:, 0:1] * bank[0, tap].astype(F32)
    for b in range(1, NB):
        total = total + weights[:, b : b + 1] * bank[b, tap].astype(F32)
    return total


def kernel_maker(latent, bank, style_w, select_w, mixed, scaled, taps, rows):
    vec = latent[...]
    expo = jnp.exp(row_dot(vec, select_w[...]))
    share = expo / jnp.sum(expo, axis=1, keepdims=True)
    style = row_dot(vec, style_w[...]) + 1.0
    style_d = down(style)
    power = jnp.zeros((1, C), F32)
    for tap in range(TAPS):
        one = weighted(bank, share, tap)
        mixed[tap] = one
        one = one * style_d
        scaled[tap] = one
        power = power + jnp.sum(one * one, axis=0, keepdims=True)
    demod = lax.rsqrt(power + EPS)
    zero = jnp.zeros((C, C), BF16)
    for line in range(4):
        for out in range(2):
            for kx in range(3):
                ky = line - out
                at = (3 * out + kx) * C
                if 0 <= ky < 3:
                    block = (scaled[3 * ky + kx] * demod).astype(BF16)
                else:
                    block = zero
                taps[line * C : line * C + C, at : at + C] = block
    rows[0:1] = style
    rows[1:2] = demod
    rows[2:3] = widen(share)
    rows[3:8] = jnp.zeros((5, C), F32)


def corr_kernel(low, block, high, noise, keep, give, acc, flat):
    height, width, _ = block.shape
    group = GROUP
    acc[...] = jnp.zeros_like(acc)
    lane = lax.broadcasted_iota(jnp.int32, (C, group * width), 1) % width

    def step(start, above, here, below):
        side = noise[pl.ds(start, group)].reshape(group * width, C).T
        zero = jnp.zeros_like(side)
        later = jnp.where(lane == width - 1, zero, pltpu.roll(side, group * width - 1, 1))
        former = jnp.where(lane == 0, zero, pltpu.roll(side, 1, 1))
        left = jnp.concatenate([later, side, former], axis=0)
        right = jnp.concatenate([above, here, below], axis=1)
        acc[...] += jnp.dot(left, right, preferred_element_type=F32)

    def lines(start):
        return block[pl.ds(start, group)].reshape(group * width, C)

    rest = (group - 1) * width
    step(
        0,
        jnp.concatenate([low[0], block[0 : group - 1].reshape(rest, C)], axis=0),
        lines(0),
        lines(1),
    )

    @pl.loop(1, height // group - 1, unroll=True)
    def _(index):
        start = index * group
        step(start, lines(start - 1), lines(start), lines(start + 1))

    start = height - group
    step(
        start,
        lines(start - 1),
        lines(start),
        jnp.concatenate([block[start + 1 : height].reshape(rest, C), high[0]], axis=0),
    )
    for ky in range(3):
        for kx in range(3):
            tap = 3 * ky + kx
            flat[tap * C : tap * C + C] = acc[kx * C : kx * C + C, ky * C : ky * C + C].T
    core = lax.axis_index("tok") % 2
    half = TAPS * C // 2
    keep[...] = flat[pl.ds(pl.multiple_of(core * half, 8), half)]
    give[...] = flat[pl.ds(pl.multiple_of((1 - core) * half, 8), half)]


def conv_kernel(low, block, high, taps, out):
    height, width, _ = block.shape
    line = lax.broadcasted_iota(jnp.int32, (width, C), 0)

    def pair(start, lines):
        left = jnp.concatenate(lines, axis=1)
        both = jnp.dot(left, taps[...], preferred_element_type=F32)
        for j in range(2):
            part = both[:, 3 * C * j : 3 * C * j + 3 * C]
            former = jnp.where(line == 0, 0.0, pltpu.roll(part[:, :C], 1, 0))
            later = jnp.where(line == width - 1, 0.0, pltpu.roll(part[:, 2 * C :], width - 1, 0))
            out[start + j] = (former + part[:, C : 2 * C] + later).astype(BF16)

    pair(0, [low[0], block[0], block[1], block[2]])

    @pl.loop(1, height // 2 - 1)
    def _(index):
        start = 2 * index
        pair(start, [block[start - 1], block[start], block[start + 1], block[start + 2]])

    start = height - 2
    pair(start, [block[start - 1], block[start], block[start + 1], high[0]])


def against_bank(bank, terms):
    sums = []
    for b in range(NB):
        total = terms[0] * bank[b, 0].astype(F32)
        for tap in range(1, TAPS):
            total = total + terms[tap] * bank[b, tap].astype(F32)
        sums.append(jnp.sum(total, axis=0, keepdims=True))
    return across(jnp.sum(jnp.concatenate(sums, axis=0), axis=1, keepdims=True))


def image_kernel(
    scale, images, mine, other, mixed, scaled, rows, latent, bank, style_w, select_w, target,
    sent, penalty, corr, proj, terms, d_scaled, d_mixed,
):
    core = lax.axis_index("tok") % 2
    half = TAPS * C // 2
    terms_flat = terms
    terms_flat[pl.ds(pl.multiple_of(core * half, 8), half)] = mine[...] * scale
    terms_flat[pl.ds(pl.multiple_of((1 - core) * half, 8), half)] = other[...] * scale
    for tap in range(TAPS):
        corr[tap] = terms_flat[tap * C : tap * C + C]
    style, demod, share = rows[0:1], rows[1:2], rows[2:3]
    style_d = down(style)
    demod3 = demod * demod * demod
    along = jnp.zeros((1, C), F32)
    for tap in range(TAPS):
        along = along + jnp.sum(corr[tap] * scaled[tap], axis=0, keepdims=True)
    pull = demod3 * along
    total = jnp.zeros((C, C), F32)
    work = terms.reshape(TAPS, C, C)
    for tap in range(TAPS):
        one = demod * corr[tap] - pull * scaled[tap]
        proj[tap] = one
        total = total + one * mixed[tap]
        work[tap] = one * style_d
    by_style = across(jnp.sum(total, axis=1, keepdims=True))
    by_share = against_bank(bank, work)
    inner = jnp.sum(share * by_share, axis=1, keepdims=True)
    by_logit = share * (by_share - inner)
    grad = row_dot_t(by_style, style_w[...]) + row_dot_t(by_logit[:, :NB], select_w[...])
    length = jnp.sqrt(jnp.sum(grad * grad, axis=1, keepdims=True) + EPS)
    gap = length - target[...]
    penalty[...] = gap * gap
    factor = (2.0 / images) * gap / length

    d_style = row_dot(grad, style_w[...])
    d_style_d = down(d_style)
    d_logit = widen(row_dot(grad, select_w[...]))
    mean = jnp.sum(share * d_logit, axis=1, keepdims=True)
    d_share = share * (d_logit - mean)
    cross = jnp.zeros((1, C), F32)
    turn = jnp.zeros((1, C), F32)
    for tap in range(TAPS):
        one = weighted(bank, d_share, tap)
        d_mixed[tap] = one
        one = one * style_d + mixed[tap] * d_style_d
        d_scaled[tap] = one
        cross = cross + jnp.sum(scaled[tap] * one, axis=0, keepdims=True)
        turn = turn + jnp.sum(corr[tap] * one, axis=0, keepdims=True)
    row_p = -demod * demod * cross
    row_d = -pull
    row_k = 2.0 * demod * demod * pull * cross - demod3 * turn
    total = jnp.zeros((C, C), F32)
    for tap in range(TAPS):
        one = row_p * proj[tap] + row_d * d_scaled[tap] + row_k * scaled[tap]
        total = total + one * mixed[tap] + proj[tap] * d_mixed[tap]
        work[tap] = one * style_d + proj[tap] * d_style_d
    to_style = across(jnp.sum(total, axis=1, keepdims=True))
    to_share = against_bank(bank, work) + by_share * (d_logit - mean) - d_logit * inner
    to_logit = share * (to_share - jnp.sum(share * to_share, axis=1, keepdims=True))

    last = jnp.concatenate(
        [
            x[:, :NB]
            for x in (
                factor * to_logit, by_logit, factor * share, factor * d_share, share, d_share,
            )
        ]
        + [jnp.zeros((1, C - 6 * NB), F32)],
        axis=1,
    )
    vec = latent[...]
    small = jnp.concatenate(
        [vec[:, C * j : C * j + C] for j in range(4)]
        + [factor * grad[:, C * j : C * j + C] for j in range(4)]
        + [factor * to_style, by_style, style, d_style, row_p, row_d, row_k, last],
        axis=0,
    )
    high = small.astype(BF16)
    lower = (small - high.astype(F32)).astype(BF16)
    width = C // images
    body = TAPS * width
    pad = sent.shape[1] - body - 32
    for s in range(images):
        pieces = [proj[tap, s * width : s * width + width] for tap in range(TAPS)]
        pieces.append(jnp.zeros((pad, C), F32))
        sent[s, : body + pad] = jnp.concatenate(pieces, axis=0).astype(BF16)
        sent[s, body + pad : body + pad + 16] = high
        sent[s, body + pad + 16 :] = lower


def final_kernel(got, bank_s, bank_grad, style_grad, select_grad, small, flip, to_k, to_dk):
    images = got.shape[0]
    width = C // images
    body = TAPS * width
    first = got.shape[1] - 32
    for n in range(images):
        small[n] = got[n, first : first + 16].astype(F32) + got[n, first + 16 :].astype(F32)
    styles = jnp.concatenate(
        [small[:, 10], small[:, 11], jnp.zeros((C - 2 * images, C), F32)], axis=0
    )
    flip[...] = styles.T
    shard = lax.axis_index("samp")
    style_c = flip[pl.ds(pl.multiple_of(shard * width, 8), width)]
    for n in range(images):
        last = small[n, 15:16]
        style = style_c[:, n : n + 1][None]
        d_style = style_c[:, images + n : images + n + 1][None]
        row_p, row_d, row_k = (small[n, j : j + 1][None] for j in (12, 13, 14))
        proj = got[n, :first].astype(F32)[:body].reshape(TAPS, width, C)
        mixed = last[:, 32:33][None] * bank_s[0]
        d_mixed = last[:, 40:41][None] * bank_s[0]
        for b in range(1, NB):
            mixed = mixed + last[:, 32 + b : 33 + b][None] * bank_s[b]
            d_mixed = d_mixed + last[:, 40 + b : 41 + b][None] * bank_s[b]
        scaled = mixed * style
        d_scaled = d_mixed * style + mixed * d_style
        second = row_p * proj + row_d * d_scaled + row_k * scaled
        to_k[n] = second * style + proj * d_style
        to_dk[n] = proj * style
    for b in range(NB):
        total = jnp.zeros((TAPS, width, C), F32)
        for n in range(images):
            last = small[n, 15:16]
            total = total + last[:, 16 + b : 17 + b][None] * to_k[n]
            total = total + last[:, 24 + b : 25 + b][None] * to_dk[n]
        bank_grad[b] = total
    last = small[:, 15]
    right = jnp.concatenate(
        [
            jnp.concatenate([small[:, 8], last], axis=1),
            jnp.concatenate([small[:, 9], pltpu.roll(last, C - NB, 1)], axis=1),
        ],
        axis=0,
    )
    for j in range(4):
        left = jnp.concatenate([small[:, j], small[:, 4 + j]], axis=0)
        both = lax.dot_general(
            left, right, (((0,), (0,)), ((), ())), precision=HIGH, preferred_element_type=F32
        )
        style_grad[C * j : C * j + C] = both[:, :C]
        select_grad[C * j : C * j + C] = both[:, C : C + NB]


def halo_rows(block):
    count = lax.axis_size("tok")
    forward = [(i, i + 1) for i in range(count - 1)]
    backward = [(i + 1, i) for i in range(count - 1)]
    rows = block.shape[0]
    low = lax.ppermute(block[rows - 1 :], "tok", forward)
    high = lax.ppermute(block[:1], "tok", backward)
    return low, high


def local(features_in, path_noise, latent, bank, style_weight, select_weight, path_mean):
    _, rows, cols, chans = features_in.shape
    images = lax.axis_size("samp")
    toks = lax.axis_size("tok")
    chips = toks // 2
    width = chans // images
    swap = [(i, i ^ 1) for i in range(toks)]
    groups = [[2 * i + c for i in range(chips)] for c in range(2)]
    scale = 1.0 / math.sqrt(rows * toks * cols)
    block, noise = features_in[0], path_noise[0]
    low, high = halo_rows(block)
    cube = (TAPS, C, C)
    mixed, scaled, taps, small = call(
        kernel_maker,
        [(cube, F32), (cube, F32), ((4 * C, 6 * C), BF16), ((8, C), F32)],
        [latent, bank, style_weight, select_weight],
        flops=2_000_000_000,
        name="kernel_maker",
    )
    half = TAPS * C // 2
    keep, give = call(
        corr_kernel,
        [((half, C), F32)] * 2,
        [low, block, high, noise],
        [pltpu.VMEM((3 * C, 3 * C), F32), pltpu.VMEM((TAPS * C, C), F32)],
        flops=4_000_000_000,
        name="corr",
    )
    keep = keep + lax.ppermute(give, "tok", swap)
    size = half // chips
    pieces = lax.all_to_all(
        keep.reshape(chips, size, C), "tok", 0, 0, axis_index_groups=groups
    )
    spread = jnp.broadcast_to(jnp.sum(pieces, axis=0)[None], (chips, size, C))
    mine = lax.all_to_all(spread, "tok", 0, 0, axis_index_groups=groups).reshape(half, C)
    other = lax.ppermute(mine, "tok", swap)
    message = -(-(TAPS * width) // 16) * 16 + 32

    def image(*refs):
        image_kernel(scale, images, *refs)

    sent, penalty = call(
        image,
        [((images, message, C), BF16), ((1, 1), F32)],
        [
            mine, other, mixed, scaled, small, latent, bank, style_weight, select_weight,
            path_mean.reshape(1, 1),
        ],
        [
            pltpu.VMEM(cube, F32),
            pltpu.VMEM(cube, F32),
            pltpu.VMEM((TAPS * C, C), F32),
            pltpu.VMEM(cube, F32),
            pltpu.VMEM(cube, F32),
        ],
        flops=6_000_000_000,
        name="image",
    )
    got = lax.all_to_all(sent, "samp", 0, 0)
    (features,) = call(
        conv_kernel,
        [((rows, cols, C), BF16)],
        [low, block, high, taps],
        flops=5_000_000_000,
        name="conv",
    )
    shard = lax.axis_index("samp")
    bank_s = lax.dynamic_slice_in_dim(bank, shard * width, width, 2).astype(F32)
    bank_grad, style_grad, select_grad = call(
        final_kernel,
        [((NB, TAPS, width, C), F32), (style_weight.shape, F32), (select_weight.shape, F32)],
        [got, bank_s],
        [
            pltpu.VMEM((images, 16, C), F32),
            pltpu.VMEM((C, C), F32),
            pltpu.VMEM((images, TAPS, width, C), F32),
            pltpu.VMEM((images, TAPS, width, C), F32),
        ],
        name="final",
    )
    return (features[None], penalty.reshape(1), bank_grad, style_grad, select_grad)


def solution(mesh):
    placed = (
        P("samp", "tok", None, None),
        P("samp", "tok", None, None),
        P("samp", None),
        P(),
        P(),
        P(),
        P(),
    )
    return jax.shard_map(
        local,
        mesh=mesh,
        in_specs=placed,
        out_specs=(P("samp", "tok", None, None), P("samp"), P(None, None, "samp", None), P(), P()),
        check_vma=False,
    )
```

time: 470 us -> 87.8 us (0.19)
  waiting for transfers between devices: 293 us -> 13 us
  matrix products: 67.1 us -> 0 us
  blocking collectives: 50.7 us -> 28.2 us
  between operations: 23.4 us -> 1.45 us
  other arithmetic: 19.4 us -> 0.99 us
  Pallas kernels: 0 us -> 17.8 us
  starting transfers between devices: 6.82 us -> 17.2 us
    psum x2 -> x0, waiting for transfers between devices: 172 us -> none  [the longest x1 141 us: local(): corr = lax.psum(corr_local, 'tok') * (1.0 / math.sqrt(height * cols))]
    reduce_scatter x1 -> x0, waiting for transfers between devices: 121 us -> none  [local(): lax.psum_scatter(bank_part, 'samp', scatter_dimension=2, tiled=True)]
    dot_general x28 -> x0, matrix products: 67.1 us -> none  [the longest x9 33.1 us: local(): jnp.einsum('nrci,nio->nrco', window, kernel_low[:, tap], preferred_elemen...]
    psum x1 -> x0, blocking collectives: 50.7 us -> none  [local(): style_grad, select_grad = lax.psum((style_part, select_part), 'samp')]
    all_to_all x0 -> x2, blocking collectives: none -> 28.2 us  [the longest x1 17.5 us: local(): lax.all_to_all(keep.reshape(chips, size, C), 'tok', 0, 0, axis_index_grou...]
    pallas_call x0 -> x5, Pallas kernels: none -> 17.8 us  [call(): pl.pallas_call(kernel, out_shape=shapes, in_specs=whole(len(inputs)), out...]
    all_to_all x0 -> x1, starting transfers between devices: none -> 8.32 us  [local(): got = lax.all_to_all(sent, 'samp', 0, 0)]
    all_to_all x0 -> x1, waiting for transfers between devices: none -> 7.04 us  [local(): got = lax.all_to_all(sent, 'samp', 0, 0)]
  transfers between devices with their start and end apart: 5 -> 5, of which waited for: 3 -> 3; matrix products, arithmetic and copies ran while one was open for 11% -> 1% of each run, Pallas kernels for 0% -> 8%
where the time goes in v1:
time: 87.8 us; the launch traced here: 87.3 us
  blocking collectives  28.2 us (32%)
  Pallas kernels  17.8 us (20%)
  starting transfers between devices  17.2 us (20%)
  waiting for transfers between devices  13 us (15%)
  local copies, waits for them, and re-layouts  8.7 us (10%)
  between operations  1.45 us (2%)
  other arithmetic  0.99 us (1%)
    pallas_call x5, Pallas kernels, call(): pl.pallas_call(kernel, out_shape=shapes, in_specs=whole(len(inputs)), out...  17.8 us
    all_to_all x1, blocking collectives, local(): lax.all_to_all(keep.reshape(chips, size, C), 'tok', 0, 0, axis_index_grou...  17.5 us
    all_to_all x1, blocking collectives, local(): lax.all_to_all(spread, 'tok', 0, 0, axis_index_groups=groups)  10.8 us
    all_to_all x1, starting transfers between devices, local(): got = lax.all_to_all(sent, 'samp', 0, 0)  8.32 us
    unnamed x20, local copies, waits for them, and re-layouts  7.69 us
    all_to_all x1, waiting for transfers between devices, local(): got = lax.all_to_all(sent, 'samp', 0, 0)  7.04 us
    ppermute x1, starting transfers between devices, halo_rows(): low = lax.ppermute(block[rows - 1:], 'tok', forward)  4.59 us
    ppermute x1, waiting for transfers between devices, halo_rows(): high = lax.ppermute(block[:1], 'tok', backward)  4.35 us
  transfers between devices with their start and end apart: 5, of which 3 were waited for; matrix products, arithmetic and copies ran while one was open for 1% of the time, Pallas kernels for 8%

profile of v1, /device:TPU:1, one launch (start us, length us, event | category | flops | bytes accessed | tf_op | source)
XLA Modules:
  0.0 87.3 jit_solution(6503834600200053522)
XLA Ops:
  0.6 1.0 %slice_bitcast_fusion = (bf16[1,512,128]{2,1,0:T(8,128)(2,1)S(1)}, bf16[1,512,128]{2,1,0:T(8,128)(2,1)S(1)}) fusion(bf16[1,16,512,128]{3,2,1,0:T(8,128)(2,1)} %param.7), kind=kLoop, calls=%fused_computation.1 | loop fusion | bytes 524288 | tf_op jit(solution)/shard_map/slice | solution.py:337
  1.6 4.6 %collective-permute-start = (bf16[1,512,128]{2,1,0:T(8,128)(2,1)S(1)}, bf16[1,512,128]{2,1,0:T(8,128)(2,1)S(1)}, u32[]{:S(2)}, u32[]{:S(2)}) collective-permute-start(bf16[1,512,128]{2,1,0:T(8,128)(2,1)S(1)} %get-tuple-element.33), channel_id=1, source_target_pairs={{0,1},{1,2},{2,3},{3,4},{4,5},{5,6},{6,7},{7,8},{8,9},{9,10},{10,1... | collective-permute-start | bytes 393224 | tf_op jit(solution)/shard_map/ppermute | solution.py:336
  6.2 1.9 %collective-permute-start.1 = (bf16[1,512,128]{2,1,0:T(8,128)(2,1)S(1)}, bf16[1,512,128]{2,1,0:T(8,128)(2,1)S(1)}, u32[]{:S(2)}, u32[]{:S(2)}) collective-permute-start(bf16[1,512,128]{2,1,0:T(8,128)(2,1)S(1)} %get-tuple-element.32), channel_id=1, source_target_pairs={{1,0},{2,1},{3,2},{4,3},{5,4},{6,5},{7,6},{8,7},{9,8},{10,9},{11,1... | collective-permute-start | bytes 393224 | tf_op jit(solution)/shard_map/ppermute | solution.py:337
  8.2 0.0 collective-permute-done.low
  8.2 4.3 %collective-permute-done.1.high = bf16[1,512,128]{2,1,0:T(8,128)(2,1)S(1)} collective-permute-done((bf16[1,512,128]{2,1,0:T(8,128)(2,1)S(1)}, bf16[1,512,128]{2,1,0:T(8,128)(2,1)S(1)}, u32[]{:S(2)}, u32[]{:S(2)}) %collective-permute-start.1) | collective-permute-done | bytes 131104 | tf_op jit(solution)/shard_map/ppermute | solution.py:337
  12.5 0.0 copy-start
  12.5 1.6 %copy-done = bf16[1,16,512,128]{3,2,1,0:T(8,128)(2,1)S(1)} copy-done((bf16[1,16,512,128]{3,2,1,0:T(8,128)(2,1)S(1)}, bf16[1,16,512,128]{3,2,1,0:T(8,128)(2,1)}, u32[]{:S(2)}) %copy-start) | copy-done | bytes 2097176
  14.1 0.0 copy-start.3
  14.1 1.6 %copy-done.3 = bf16[1,16,512,128]{3,2,1,0:T(8,128)(2,1)S(1)} copy-done((bf16[1,16,512,128]{3,2,1,0:T(8,128)(2,1)S(1)}, bf16[1,16,512,128]{3,2,1,0:T(8,128)(2,1)}, u32[]{:S(2)}) %copy-start.3) | copy-done | bytes 2097176
  15.7 3.9 %corr.1 = (f32[576,128]{1,0:T(8,128)S(1)}, f32[576,128]{1,0:T(8,128)S(1)}) custom-call(bf16[1,512,128]{2,1,0:T(8,128)(2,1)S(1)} %collective-permute-done.low, bf16[16,512,128]{2,1,0:T(8,128)(2,1)S(1)} %bitcast.14, bf16[1,512,128]{2,1,0:T(8,128)(2,1)S(1)} %collective-permute-done.1.high, bf16[16,512,128]{2,1,0:T(8,128)(2,1)S(1)} %bitcast.16), custom_call_target="tpu_custom_call" | custom-call | flops 4000000000 | bytes 4456448 | tf_op jit(solution)/shard_map/corr/pallas_call | solution.py:28
  19.6 0.0 copy-start.8
  19.6 0.0 copy-start.4
  19.6 0.0 copy-start.5
  19.6 0.1 collective-permute-start.2
  19.7 1.6 %collective-permute-done.2 = f32[576,128]{1,0:T(8,128)S(1)} collective-permute-done((f32[576,128]{1,0:T(8,128)S(1)}, f32[576,128]{1,0:T(8,128)S(1)}, u32[]{:S(2)}, u32[]{:S(2)}) %collective-permute-start.2) | collective-permute-done | bytes 294944 | tf_op jit(solution)/shard_map/ppermute | solution.py:369
  21.3 17.5 %all_to_all.15 = f32[8,72,128]{2,1,0:T(8,128)S(1)} all-to-all(f32[8,72,128]{2,1,0:T(8,128)S(1)} %bitcast.17), channel_id=1, replica_groups={{0,2,4,6,8,10,12,14},{1,3,5,7,9,11,13,15},{16,18,20,22,24,26,28,30},{17..., dimensions={0} | all-to-all | bytes 589824 | tf_op jit(solution)/shard_map/all_to_all | solution.py:371
  38.8 10.8 %all_to_all.16 = f32[8,72,128]{2,1,0:T(8,128)S(1)} all-to-all(f32[8,72,128]{2,1,0:T(8,128)S(1)} %broadcast_in_dim.10), channel_id=1, replica_groups={{0,2,4,6,8,10,12,14},{1,3,5,7,9,11,13,15},{16,18,20,22,24,26,28,30},{17..., dimensions={0} | all-to-all | bytes 589824 | tf_op jit(solution)/shard_map/all_to_all | solution.py:375
  49.6 2.3 %collective-permute-start.3 = (f32[576,128]{1,0:T(8,128)S(1)}, f32[576,128]{1,0:T(8,128)S(1)}, u32[]{:S(2)}, u32[]{:S(2)}) collective-permute-start(f32[576,128]{1,0:T(8,128)S(1)} %bitcast.12), channel_id=1, source_target_pairs={{0,1},{1,0},{2,3},{3,2},{4,5},{5,4},{6,7},{7,6},{8,9},{9,8},{10,11... | collective-permute-start | bytes 884744 | tf_op jit(solution)/shard_map/ppermute | solution.py:376
  51.8 0.0 copy-done.8
  51.8 0.1 copy.12.select_w.refs_8_
  52.6 0.0 copy-done.4
  52.6 0.0 copy-done.5
  52.6 0.0 copy-start.2
  52.6 1.7 %copy-done.2 = bf16[8,9,128,128]{3,2,1,0:T(8,128)(2,1)S(1)} copy-done((bf16[8,9,128,128]{3,2,1,0:T(8,128)(2,1)S(1)}, bf16[8,9,128,128]{3,2,1,0:T(8,128)(2,1)}, u32[]{:S(2)}) %copy-start.2) | copy-done | bytes 2359320
  54.3 1.2 %kernel_maker.1 = (f32[9,128,128]{2,1,0:T(8,128)S(1)}, f32[9,128,128]{2,1,0:T(8,128)S(1)}, bf16[512,768]{1,0:T(8,128)(2,1)S(1)}, f32[8,128]{1,0:T(8,128)S(1)}) custom-call(f32[1,512]{1,0:T(1,128)S(1)} %copy-done.5, bf16[8,9,128,128]{3,2,1,0:T(8,128)(2,1)S(1)} %copy-done.2, f32[512,128]{1,0:T(8,128)S(1)} %copy-done.4, f32[512,8]{1,0:T(8,128)S(1)} %copy.12.select_w.refs_8_), custom_call_target="tpu_custom_call" | custom-call | flops 2000000000 | bytes 2639872 | tf_op jit(solution)/shard_map/kernel_maker/pallas_call | solution.py:28
  55.5 0.0 copy-start.6
  55.5 0.9 copy-done.6
  56.3 0.0 collective-permute-done.3.refs_1_
  56.4 0.0 copy-start.1
  56.4 4.2 %image.1 = (bf16[16,112,128]{2,1,0:T(8,128)(2,1)}, f32[1,1]{1,0:T(1,128)}) custom-call(f32[576,128]{1,0:T(8,128)S(1)} %bitcast.13, f32[576,128]{1,0:T(8,128)S(1)} %collective-permute-done.3.refs_1_, f32[9,128,128]{2,1,0:T(8,128)S(1)} %get-tuple-element.19.refs_2_, f32[9,128,128]{2,1,0:T(8,128)S(1)} %get-tuple-element.20.refs_3_, ...), custom_call_target="tpu_custom_call" | custom-call | flops 6000000000 | bytes 4413444 | tf_op jit(solution)/shard_map/image/pallas_call | solution.py:28
  60.5 8.3 %all-to-all-start.2 = ((bf16[16,112,128]{2,1,0:T(8,128)(2,1)}), bf16[16,112,128]{2,1,0:T(8,128)(2,1)S(1)}, u32[]{:S(2)}, u32[]{:S(2)}) async-start(bf16[16,112,128]{2,1,0:T(8,128)(2,1)} %get-tuple-element.23), calls=%async_computation.2 | async-start | bytes 917504 | tf_op jit(solution)/shard_map/all_to_all | solution.py:399
  68.9 0.9 %dynamic-slice_convert_fusion.bank_s = f32[8,9,8,128]{3,2,1,0:T(8,128)S(1)} fusion(bf16[8,9,128,128]{3,2,1,0:T(8,128)(2,1)} %refs_6_.1, s32[]{:T(128)S(6)} %select_n.3), kind=kLoop, calls=%fused_computation | loop fusion | flops 73728 | bytes 442372 | tf_op jit(solution)/shard_map/convert_element_type | solution.py:408
  69.8 0.0 copy-done.1
  69.8 0.0 copy-start.7
  69.8 1.1 %copy-done.7 = bf16[512,768]{1,0:T(8,128)(2,1)S(1)} copy-done((bf16[512,768]{1,0:T(8,128)(2,1)S(1)}, bf16[512,768]{1,0:T(8,128)(2,1)}, u32[]{:S(2)}) %copy-start.7) | copy-done | bytes 786456
  71.0 5.9 %conv.1 = bf16[16,512,128]{2,1,0:T(8,128)(2,1)} custom-call(bf16[1,512,128]{2,1,0:T(8,128)(2,1)S(1)} %collective-permute-done.low, bf16[16,512,128]{2,1,0:T(8,128)(2,1)S(1)} %bitcast.15, bf16[1,512,128]{2,1,0:T(8,128)(2,1)S(1)} %collective-permute-done.1.high, bf16[512,768]{1,0:T(8,128)(2,1)S(1)} %copy-done.7), custom_call_target="tpu_custom_call" | custom-call | flops 5000000000 | bytes 3145728 | tf_op jit(solution)/shard_map/conv/pallas_call | solution.py:28
  76.9 7.0 %all-to-all-done.2.got = bf16[16,112,128]{2,1,0:T(8,128)(2,1)S(1)} async-done(((bf16[16,112,128]{2,1,0:T(8,128)(2,1)}), bf16[16,112,128]{2,1,0:T(8,128)(2,1)S(1)}, u32[]{:S(2)}, u32[]{:S(2)}) %all-to-all-start.2) | async-done | bytes 458784 | tf_op jit(solution)/shard_map/all_to_all | solution.py:399
  84.0 2.6 %final.1 = (f32[8,9,8,128]{3,2,1,0:T(8,128)}, f32[512,128]{1,0:T(8,128)}, f32[512,8]{1,0:T(8,128)S(1)}) custom-call(bf16[16,112,128]{2,1,0:T(8,128)(2,1)S(1)} %all-to-all-done.2.got, f32[8,9,8,128]{3,2,1,0:T(8,128)S(1)} %dynamic-slice_convert_fusion.bank_s), custom_call_target="tpu_custom_call" | custom-call | bytes 753664 | tf_op jit(solution)/shard_map/final/pallas_call | solution.py:28
  86.6 0.7 copy.14
  (3 shorter events, 0.1 us)
Async XLA Ops:
  1.6 6.5 %collective-permute-start = (bf16[1,512,128]{2,1,0:T(8,128)(2,1)S(1)}, bf16[1,512,128]{2,1,0:T(8,128)(2,1)S(1)}, u32[]{:S(2)}, u32[]{:S(2)}) collective-permute-start(bf16[1,512,128]{2,1,0:T(8,128)(2,1)S(1)} %get-tuple-element.33), channel_id=1, source_target_pairs={{0,1},{1,2},{2,3},{3,4},{4,5},{5,6},{6,7},{7,8},{8,9},{9,10},{10,1... | collective-permute-start | bytes 393224 | tf_op jit(solution)/shard_map/ppermute | solution.py:336
  6.2 6.3 %collective-permute-start.1 = (bf16[1,512,128]{2,1,0:T(8,128)(2,1)S(1)}, bf16[1,512,128]{2,1,0:T(8,128)(2,1)S(1)}, u32[]{:S(2)}, u32[]{:S(2)}) collective-permute-start(bf16[1,512,128]{2,1,0:T(8,128)(2,1)S(1)} %get-tuple-element.32), channel_id=1, source_target_pairs={{1,0},{2,1},{3,2},{4,3},{5,4},{6,5},{7,6},{8,7},{9,8},{10,9},{11,1... | collective-permute-start | bytes 393224 | tf_op jit(solution)/shard_map/ppermute | solution.py:337
  12.5 1.6 %copy-start = (bf16[1,16,512,128]{3,2,1,0:T(8,128)(2,1)S(1)}, bf16[1,16,512,128]{3,2,1,0:T(8,128)(2,1)}, u32[]{:S(2)}) copy-start(bf16[1,16,512,128]{3,2,1,0:T(8,128)(2,1)} %param.7) | copy-start | bytes 6291460
  14.1 1.6 %copy-start.3 = (bf16[1,16,512,128]{3,2,1,0:T(8,128)(2,1)S(1)}, bf16[1,16,512,128]{3,2,1,0:T(8,128)(2,1)}, u32[]{:S(2)}) copy-start(bf16[1,16,512,128]{3,2,1,0:T(8,128)(2,1)} %param.8) | copy-start | bytes 6291460
  19.6 32.3 %copy-start.8 = (f32[512,8]{0,1:T(8,128)S(1)}, f32[512,8]{0,1:T(8,128)}, u32[]{:S(2)}) copy-start(f32[512,8]{0,1:T(8,128)} %param.12) | copy-start | bytes 49156
  19.6 33.1 %copy-start.4 = (f32[512,128]{1,0:T(8,128)S(1)}, f32[512,128]{1,0:T(8,128)}, u32[]{:S(2)}) copy-start(f32[512,128]{1,0:T(8,128)} %refs_7_.1) | copy-start | bytes 786436
  19.6 33.1 %copy-start.5 = (f32[1,512]{1,0:T(1,128)S(1)}, f32[1,512]{1,0:T(1,128)}, u32[]{:S(2)}) copy-start(f32[1,512]{1,0:T(1,128)} %refs_5_.1) | copy-start | bytes 6148
  19.6 1.7 %collective-permute-start.2 = (f32[576,128]{1,0:T(8,128)S(1)}, f32[576,128]{1,0:T(8,128)S(1)}, u32[]{:S(2)}, u32[]{:S(2)}) collective-permute-start(f32[576,128]{1,0:T(8,128)S(1)} %get-tuple-element.18), channel_id=1, source_target_pairs={{0,1},{1,0},{2,3},{3,2},{4,5},{5,4},{6,7},{7,6},{8,9},{9,8},{10,11... | collective-permute-start | bytes 884744 | tf_op jit(solution)/shard_map/ppermute | solution.py:369
  49.6 6.8 %collective-permute-start.3 = (f32[576,128]{1,0:T(8,128)S(1)}, f32[576,128]{1,0:T(8,128)S(1)}, u32[]{:S(2)}, u32[]{:S(2)}) collective-permute-start(f32[576,128]{1,0:T(8,128)S(1)} %bitcast.12), channel_id=1, source_target_pairs={{0,1},{1,0},{2,3},{3,2},{4,5},{5,4},{6,7},{7,6},{8,9},{9,8},{10,11... | collective-permute-start | bytes 884744 | tf_op jit(solution)/shard_map/ppermute | solution.py:376
  52.6 1.7 %copy-start.2 = (bf16[8,9,128,128]{3,2,1,0:T(8,128)(2,1)S(1)}, bf16[8,9,128,128]{3,2,1,0:T(8,128)(2,1)}, u32[]{:S(2)}) copy-start(bf16[8,9,128,128]{3,2,1,0:T(8,128)(2,1)} %refs_6_.1) | copy-start | bytes 7077892
  55.5 0.9 %copy-start.6 = (bf16[512,768]{1,0:T(8,128)(2,1)}, bf16[512,768]{1,0:T(8,128)(2,1)S(1)}, u32[]{:S(2)}) copy-start(bf16[512,768]{1,0:T(8,128)(2,1)S(1)} %get-tuple-element.16.taps) | copy-start | bytes 2359300
  56.4 13.5 %copy-start.1 = (bf16[1,16,512,128]{3,2,1,0:T(8,128)(2,1)S(1)}, bf16[1,16,512,128]{3,2,1,0:T(8,128)(2,1)}, u32[]{:S(2)}) copy-start(bf16[1,16,512,128]{3,2,1,0:T(8,128)(2,1)} %param.7) | copy-start | bytes 6291460
  60.5 23.4 %all-to-all-start.2 = ((bf16[16,112,128]{2,1,0:T(8,128)(2,1)}), bf16[16,112,128]{2,1,0:T(8,128)(2,1)S(1)}, u32[]{:S(2)}, u32[]{:S(2)}) async-start(bf16[16,112,128]{2,1,0:T(8,128)(2,1)} %get-tuple-element.23), calls=%async_computation.2 | async-start | bytes 917504 | tf_op jit(solution)/shard_map/all_to_all | solution.py:399
  69.8 1.1 %copy-start.7 = (bf16[512,768]{1,0:T(8,128)(2,1)S(1)}, bf16[512,768]{1,0:T(8,128)(2,1)}, u32[]{:S(2)}) copy-start(bf16[512,768]{1,0:T(8,128)(2,1)} %copy-done.6) | copy-start | bytes 2359300

commit v2 on v1

--- a/solution.py
+++ b/solution.py
@@ -15,6 +15,7 @@
 C = 128
 NB = 8
 GROUP = 4
+CORR_LIMIT = 61
 MIB = 1024 * 1024
 
 
@@ -22,13 +23,16 @@
     return [pl.BlockSpec(memory_space=pltpu.VMEM)] * count
 
 
-def call(kernel, outs, inputs, scratch=(), limit=24, flops=0, name=None):
+def call(kernel, outs, inputs, scratch=(), limit=10, flops=0, name=None, far=()):
+    specs = whole(len(inputs))
+    for place in far:
+        specs[place] = pl.BlockSpec(memory_space=pltpu.HBM)
     size = sum(math.prod(x.shape) * x.dtype.itemsize for x in inputs)
     shapes = [jax.ShapeDtypeStruct(s, d) for s, d in outs]
     return pl.pallas_call(
         kernel,
         out_shape=shapes,
-        in_specs=whole(len(inputs)),
+        in_specs=specs,
         out_specs=whole(len(outs)),
         scratch_shapes=list(scratch),
         compiler_params=pltpu.CompilerParams(vmem_limit_bytes=limit * MIB),
@@ -71,17 +75,15 @@
     return total
 
 
-def kernel_maker(latent, bank, style_w, select_w, mixed, scaled, taps, rows):
+def kernel_maker(latent, bank, style_w, select_w, taps, rows, scaled):
     vec = latent[...]
-    expo = jnp.exp(row_dot(vec, select_w[...]))
+    expo = jnp.exp(row_dot_t(vec, select_w[...]))
     share = expo / jnp.sum(expo, axis=1, keepdims=True)
     style = row_dot(vec, style_w[...]) + 1.0
     style_d = down(style)
     power = jnp.zeros((1, C), F32)
     for tap in range(TAPS):
-        one = weighted(bank, share, tap)
-        mixed[tap] = one
-        one = one * style_d
+        one = weighted(bank, share, tap) * style_d
         scaled[tap] = one
         power = power + jnp.sum(one * one, axis=0, keepdims=True)
     demod = lax.rsqrt(power + EPS)
@@ -102,11 +104,29 @@
     rows[3:8] = jnp.zeros((5, C), F32)
 
 
-def corr_kernel(low, block, high, noise, keep, give, acc, flat):
+def corr_kernel(block_far, noise_far, flat, edge_low, edge_high, acc, block, noise, sems):
     height, width, _ = block.shape
     group = GROUP
+    count = height // group
+
+    def fetch(which, index):
+        source, target = ((block_far, block), (noise_far, noise))[which]
+        part = pl.ds(index * group, group)
+        return pltpu.make_async_copy(source.at[part], target.at[part], sems.at[which, index])
+
+    fetch(0, 0).start()
+    for index in range(count):
+        if index + 1 < count:
+            fetch(0, index + 1).start()
+        fetch(1, index).start()
+    fetch(0, 0).wait()
     acc[...] = jnp.zeros_like(acc)
     lane = lax.broadcasted_iota(jnp.int32, (C, group * width), 1) % width
+
+    def ready(index):
+        if index + 1 < count:
+            fetch(0, index + 1).wait()
+        fetch(1, index).wait()
 
     def step(start, above, here, below):
         side = noise[pl.ds(start, group)].reshape(group * width, C).T
@@ -116,62 +136,145 @@
         left = jnp.concatenate([later, side, former], axis=0)
         right = jnp.concatenate([above, here, below], axis=1)
         acc[...] += jnp.dot(left, right, preferred_element_type=F32)
+        return left
 
     def lines(start):
         return block[pl.ds(start, group)].reshape(group * width, C)
 
     rest = (group - 1) * width
-    step(
+    none = jnp.zeros((width, C), BF16)
+    ready(0)
+    left = step(
         0,
-        jnp.concatenate([low[0], block[0 : group - 1].reshape(rest, C)], axis=0),
+        jnp.concatenate([none, block[0 : group - 1].reshape(rest, C)], axis=0),
         lines(0),
         lines(1),
     )
-
-    @pl.loop(1, height // group - 1, unroll=True)
-    def _(index):
+    edge_low[...] = left[:, :width]
+
+    for index in range(1, count - 1):
+        ready(index)
         start = index * group
         step(start, lines(start - 1), lines(start), lines(start + 1))
 
     start = height - group
-    step(
+    ready(count - 1)
+    left = step(
         start,
         lines(start - 1),
         lines(start),
-        jnp.concatenate([block[start + 1 : height].reshape(rest, C), high[0]], axis=0),
-    )
+        jnp.concatenate([block[start + 1 : height].reshape(rest, C), none], axis=0),
+    )
+    edge_high[...] = left[:, rest:]
     for ky in range(3):
         for kx in range(3):
             tap = 3 * ky + kx
             flat[tap * C : tap * C + C] = acc[kx * C : kx * C + C, ky * C : ky * C + C].T
+
+
+def edge_kernel(near, far, flat, edge_low, edge_high, rows, keep, give, both):
     core = lax.axis_index("tok") % 2
+    first = jnp.where(core == 0, far[0], near[0])
+    last = jnp.where(core == 0, near[0], far[0])
+    above = jnp.dot(edge_low[...], first, preferred_element_type=F32)
+    below = jnp.dot(edge_high[...], last, preferred_element_type=F32)
+    side = 3 * C
+    both[side : 2 * side] = flat[side : 2 * side]
+    for kx in range(3):
+        at = kx * C
+        both[at : at + C] = flat[at : at + C] + above[at : at + C].T
+        low = 2 * side + at
+        both[low : low + C] = flat[low : low + C] + below[at : at + C].T
     half = TAPS * C // 2
-    keep[...] = flat[pl.ds(pl.multiple_of(core * half, 8), half)]
-    give[...] = flat[pl.ds(pl.multiple_of((1 - core) * half, 8), half)]
-
-
-def conv_kernel(low, block, high, taps, out):
-    height, width, _ = block.shape
+    keep[...] = both[pl.ds(pl.multiple_of(core * half, 8), half)]
+    give[...] = both[pl.ds(pl.multiple_of((1 - core) * half, 8), half)]
+
+
+def conv_kernel(offset, pairs, final, near, far, above, lines, below, taps, *rest):
+    out, token = rest[-2:]
+    token[...] = jnp.zeros_like(token)
+    width = lines.shape[1]
     line = lax.broadcasted_iota(jnp.int32, (width, C), 0)
-
-    def pair(start, lines):
-        left = jnp.concatenate(lines, axis=1)
-        both = jnp.dot(left, taps[...], preferred_element_type=F32)
-        for j in range(2):
-            part = both[:, 3 * C * j : 3 * C * j + 3 * C]
-            former = jnp.where(line == 0, 0.0, pltpu.roll(part[:, :C], 1, 0))
-            later = jnp.where(line == width - 1, 0.0, pltpu.roll(part[:, 2 * C :], width - 1, 0))
-            out[start + j] = (former + part[:, C : 2 * C] + later).astype(BF16)
-
-    pair(0, [low[0], block[0], block[1], block[2]])
-
-    @pl.loop(1, height // 2 - 1)
-    def _(index):
-        start = 2 * index
-        pair(start, [block[start - 1], block[start], block[start + 1], block[start + 2]])
-
-    start = height - 2
-    pair(start, [block[start - 1], block[start], block[start + 1], high[0]])
+    core = lax.axis_index("tok") % 2
+    place = offset + pl.program_id(0)
+    first, last = above[0], below[0]
+    if offset == 0:
+        first = jnp.where(place == 0, jnp.where(core == 0, far[0], near[0]), first)
+    if final:
+        last = jnp.where(place == pairs - 1, jnp.where(core == 0, near[0], far[0]), last)
+    left = jnp.concatenate([first, lines[0], lines[1], last], axis=1)
+    both = jnp.dot(left, taps[...], preferred_element_type=F32)
+    for j in range(2):
+        part = both[:, 3 * C * j : 3 * C * j + 3 * C]
+        former = jnp.where(line == 0, 0.0, pltpu.roll(part[:, :C], 1, 0))
+        later = jnp.where(line == width - 1, 0.0, pltpu.roll(part[:, 2 * C :], width - 1, 0))
+        out[j] = (former + part[:, C : 2 * C] + later).astype(BF16)
+
+
+def conv_part(offset, steps, near, far, block, taps, after, done):
+    rows, cols, _ = block.shape
+    pairs = rows // 2
+    one = (1, cols, C)
+
+    def body(*refs):
+        conv_kernel(offset, pairs, offset + steps == pairs, *refs)
+
+    specs = [
+        pl.BlockSpec(one, lambda g: (0, 0, 0)),
+        pl.BlockSpec(one, lambda g: (0, 0, 0)),
+        pl.BlockSpec(one, lambda g: (jnp.maximum(2 * (offset + g) - 1, 0), 0, 0)),
+        pl.BlockSpec((2, cols, C), lambda g: (offset + g, 0, 0)),
+        pl.BlockSpec(one, lambda g: (jnp.minimum(2 * (offset + g) + 2, rows - 1), 0, 0)),
+        pl.BlockSpec(taps.shape, lambda g: (0, 0)),
+        pl.BlockSpec(memory_space=pl.ANY),
+    ]
+    inputs = [near, far, block, block, block, taps, after]
+    aliases = {}
+    if done is not None:
+        aliases = {len(inputs): 0}
+        specs.append(pl.BlockSpec(memory_space=pl.ANY))
+        inputs.append(done)
+    return pl.pallas_call(
+        body,
+        grid=(steps,),
+        out_shape=[
+            jax.ShapeDtypeStruct((rows, cols, C), BF16),
+            jax.ShapeDtypeStruct((8, C), F32),
+        ],
+        in_specs=specs,
+        out_specs=[
+            pl.BlockSpec((2, cols, C), lambda g: (offset + g, 0, 0)),
+            pl.BlockSpec((8, C), lambda g: (0, 0)),
+        ],
+        input_output_aliases=aliases,
+        compiler_params=pltpu.CompilerParams(vmem_limit_bytes=10 * MIB),
+        cost_estimate=pl.CostEstimate(
+            flops=steps * 600_000_000, bytes_accessed=steps * 900_000, transcendentals=0
+        ),
+        name="conv",
+    )(*inputs)
+
+
+def split_kernel(keep, given, own, first, second, third):
+    place = lax.axis_index("tok") // 2 % 4
+    size = own.shape[0]
+    for step, out in enumerate((own, first, second, third)):
+        part = pl.ds(pl.multiple_of((place + step) % 4 * size, 8), size)
+        out[...] = keep[part] + given[part]
+
+
+def add_kernel(*refs):
+    total = refs[0][...]
+    for ref in refs[1:-2]:
+        total = total + ref[...]
+    refs[-1][...] = total
+
+
+def gather_kernel(own, first, second, third, after, out):
+    place = lax.axis_index("tok") // 2 % 4
+    size = own.shape[0]
+    for step, part in enumerate((own, first, second, third)):
+        out[pl.ds(pl.multiple_of((place - step + 4) % 4 * size, 8), size)] = part[...]
 
 
 def against_bank(bank, terms):
@@ -185,8 +288,8 @@
 
 
 def image_kernel(
-    scale, images, mine, other, mixed, scaled, rows, latent, bank, style_w, select_w, target,
-    sent, penalty, corr, proj, terms, d_scaled, d_mixed,
+    scale, images, mine, other, rows, latent, bank, style_w, select_w, target,
+    after, sent, penalty, corr, proj, terms, d_scaled, d_mixed, mixed, scaled,
 ):
     core = lax.axis_index("tok") % 2
     half = TAPS * C // 2
@@ -200,7 +303,11 @@
     demod3 = demod * demod * demod
     along = jnp.zeros((1, C), F32)
     for tap in range(TAPS):
-        along = along + jnp.sum(corr[tap] * scaled[tap], axis=0, keepdims=True)
+        one = weighted(bank, share, tap)
+        mixed[tap] = one
+        one = one * style_d
+        scaled[tap] = one
+        along = along + jnp.sum(corr[tap] * one, axis=0, keepdims=True)
     pull = demod3 * along
     total = jnp.zeros((C, C), F32)
     work = terms.reshape(TAPS, C, C)
@@ -213,7 +320,7 @@
     by_share = against_bank(bank, work)
     inner = jnp.sum(share * by_share, axis=1, keepdims=True)
     by_logit = share * (by_share - inner)
-    grad = row_dot_t(by_style, style_w[...]) + row_dot_t(by_logit[:, :NB], select_w[...])
+    grad = row_dot_t(by_style, style_w[...]) + row_dot(by_logit[:, :NB], select_w[...])
     length = jnp.sqrt(jnp.sum(grad * grad, axis=1, keepdims=True) + EPS)
     gap = length - target[...]
     penalty[...] = gap * gap
@@ -221,7 +328,7 @@
 
     d_style = row_dot(grad, style_w[...])
     d_style_d = down(d_style)
-    d_logit = widen(row_dot(grad, select_w[...]))
+    d_logit = widen(row_dot_t(grad, select_w[...]))
     mean = jnp.sum(share * d_logit, axis=1, keepdims=True)
     d_share = share * (d_logit - mean)
     cross = jnp.zeros((1, C), F32)
@@ -265,23 +372,36 @@
     high = small.astype(BF16)
     lower = (small - high.astype(F32)).astype(BF16)
     width = C // images
-    body = TAPS * width
-    pad = sent.shape[1] - body - 32
-    for s in range(images):
-        pieces = [proj[tap, s * width : s * width + width] for tap in range(TAPS)]
-        pieces.append(jnp.zeros((pad, C), F32))
-        sent[s, : body + pad] = jnp.concatenate(pieces, axis=0).astype(BF16)
-        sent[s, body + pad : body + pad + 16] = high
-        sent[s, body + pad + 16 :] = lower
-
-
-def final_kernel(got, bank_s, bank_grad, style_grad, select_grad, small, flip, to_k, to_dk):
-    images = got.shape[0]
+    size = sent.shape[1]
+    split = size // width
+
+    def slices(taps, s):
+        return jnp.concatenate([proj[tap, s * width : s * width + width] for tap in taps], axis=0)
+
+    @pl.when(core == 0)
+    def _():
+        for s in range(images):
+            sent[s] = slices(range(split), s).astype(BF16)
+
+    @pl.when(core == 1)
+    def _():
+        none = jnp.zeros((size - 32 - (TAPS - split) * width, C), F32)
+        for s in range(images):
+            body = jnp.concatenate([slices(range(split, TAPS), s), none], axis=0)
+            sent[s] = jnp.concatenate([high, lower, body.astype(BF16)], axis=0)
+
+
+def final_kernel(
+    mine, other, bank_s, bank_grad, style_grad, select_grad, got, small, flip, to_k, to_dk
+):
+    images, size, _ = mine.shape
     width = C // images
-    body = TAPS * width
-    first = got.shape[1] - 32
+    split = size // width
+    core = lax.axis_index("tok") % 2
+    got[core] = mine[...]
+    got[1 - core] = other[...]
     for n in range(images):
-        small[n] = got[n, first : first + 16].astype(F32) + got[n, first + 16 :].astype(F32)
+        small[n] = got[1, n, :16].astype(F32) + got[1, n, 16:32].astype(F32)
     styles = jnp.concatenate(
         [small[:, 10], small[:, 11], jnp.zeros((C - 2 * images, C), F32)], axis=0
     )
@@ -293,7 +413,8 @@
         style = style_c[:, n : n + 1][None]
         d_style = style_c[:, images + n : images + n + 1][None]
         row_p, row_d, row_k = (small[n, j : j + 1][None] for j in (12, 13, 14))
-        proj = got[n, :first].astype(F32)[:body].reshape(TAPS, width, C)
+        rest = got[1, n, 32:].astype(F32)[: (TAPS - split) * width]
+        proj = jnp.concatenate([got[0, n].astype(F32), rest], axis=0).reshape(TAPS, width, C)
         mixed = last[:, 32:33][None] * bank_s[0]
         d_mixed = last[:, 40:41][None] * bank_s[0]
         for b in range(1, NB):
@@ -325,56 +446,87 @@
             left, right, (((0,), (0,)), ((), ())), precision=HIGH, preferred_element_type=F32
         )
         style_grad[C * j : C * j + C] = both[:, :C]
-        select_grad[C * j : C * j + C] = both[:, C : C + NB]
-
-
-def halo_rows(block):
+        select_grad[:, C * j : C * j + C] = both[:, C:].T[:NB]
+
+
+def neighbour_rows(block):
     count = lax.axis_size("tok")
-    forward = [(i, i + 1) for i in range(count - 1)]
-    backward = [(i + 1, i) for i in range(count - 1)]
-    rows = block.shape[0]
-    low = lax.ppermute(block[rows - 1 :], "tok", forward)
-    high = lax.ppermute(block[:1], "tok", backward)
-    return low, high
+    core = lax.axis_index("tok") % 2
+    first, last = block[:1], block[block.shape[0] - 1 :]
+    swap = [(i, i ^ 1) for i in range(count)]
+    pairs = [(i, i + 1) for i in range(1, count - 1, 2)]
+    pairs = pairs + [(b, a) for a, b in pairs]
+    far = lax.ppermute(jnp.where(core == 0, first, last), "tok", pairs)
+    near = lax.ppermute(jnp.where(core == 0, last, first), "tok", swap)
+    return near, far
 
 
 def local(features_in, path_noise, latent, bank, style_weight, select_weight, path_mean):
     _, rows, cols, chans = features_in.shape
     images = lax.axis_size("samp")
     toks = lax.axis_size("tok")
-    chips = toks // 2
     width = chans // images
     swap = [(i, i ^ 1) for i in range(toks)]
-    groups = [[2 * i + c for i in range(chips)] for c in range(2)]
     scale = 1.0 / math.sqrt(rows * toks * cols)
     block, noise = features_in[0], path_noise[0]
-    low, high = halo_rows(block)
+    near, far = neighbour_rows(block)
     cube = (TAPS, C, C)
-    mixed, scaled, taps, small = call(
+    select_t = select_weight.T
+    taps, small = call(
         kernel_maker,
-        [(cube, F32), (cube, F32), ((4 * C, 6 * C), BF16), ((8, C), F32)],
-        [latent, bank, style_weight, select_weight],
+        [((4 * C, 6 * C), BF16), ((8, C), F32)],
+        [latent, bank, style_weight, select_t],
+        [pltpu.VMEM(cube, F32)],
         flops=2_000_000_000,
         name="kernel_maker",
     )
     half = TAPS * C // 2
-    keep, give = call(
+    edge = ((3 * C, cols), BF16)
+    flat, edge_low, edge_high = call(
         corr_kernel,
-        [((half, C), F32)] * 2,
-        [low, block, high, noise],
-        [pltpu.VMEM((3 * C, 3 * C), F32), pltpu.VMEM((TAPS * C, C), F32)],
+        [((TAPS * C, C), F32), edge, edge],
+        [block, noise],
+        [
+            pltpu.VMEM((3 * C, 3 * C), F32),
+            pltpu.VMEM(block.shape, BF16),
+            pltpu.VMEM(noise.shape, BF16),
+            pltpu.SemaphoreType.DMA((2, rows // GROUP)),
+        ],
         flops=4_000_000_000,
         name="corr",
-    )
-    keep = keep + lax.ppermute(give, "tok", swap)
-    size = half // chips
-    pieces = lax.all_to_all(
-        keep.reshape(chips, size, C), "tok", 0, 0, axis_index_groups=groups
-    )
-    spread = jnp.broadcast_to(jnp.sum(pieces, axis=0)[None], (chips, size, C))
-    mine = lax.all_to_all(spread, "tok", 0, 0, axis_index_groups=groups).reshape(half, C)
+        far=(0, 1),
+        limit=CORR_LIMIT,
+    )
+    keep, give = call(
+        edge_kernel,
+        [((half, C), F32)] * 2,
+        [near, far, flat, edge_low, edge_high, small],
+        [pltpu.VMEM((TAPS * C, C), F32)],
+        flops=500_000_000,
+        name="edge",
+    )
+    given = lax.ppermute(give, "tok", swap)
+    quarter = ((half // 4, C), F32)
+
+    def along_y(step):
+        return [(i, i // 8 * 8 + (i + 2 * step) % 8) for i in range(toks)]
+
+    own, *out = call(split_kernel, [quarter] * 4, [keep, given], name="split")
+    features, token = conv_part(0, 3, near, far, block, taps, own, None)
+    came = [lax.ppermute(x, "tok", along_y(j + 1)) for j, x in enumerate(out)]
+    (own,) = call(add_kernel, [quarter], [own, *came, token], name="add_y")
+    features, token = conv_part(3, 2, near, far, block, taps, own, features)
+    came = lax.ppermute(own, "tok", [(i, i ^ 8) for i in range(toks)])
+    (own,) = call(add_kernel, [quarter], [own, came, token], name="add_x")
+    features, token = conv_part(5, 3, near, far, block, taps, own, features)
+    came = [lax.ppermute(own, "tok", along_y(j)) for j in (1, 2, 3)]
+    (mine,) = call(
+        gather_kernel, [((half, C), F32)], [own, *came, token], name="gather_y"
+    )
     other = lax.ppermute(mine, "tok", swap)
-    message = -(-(TAPS * width) // 16) * 16 + 32
+    shard = lax.axis_index("samp")
+    bank_s = lax.dynamic_slice_in_dim(bank, shard * width, width, 2).astype(F32)
+    message = (TAPS - 1) * width
 
     def image(*refs):
         image_kernel(scale, images, *refs)
@@ -383,8 +535,8 @@
         image,
         [((images, message, C), BF16), ((1, 1), F32)],
         [
-            mine, other, mixed, scaled, small, latent, bank, style_weight, select_weight,
-            path_mean.reshape(1, 1),
+            mine, other, small, latent, bank, style_weight, select_t,
+            path_mean.reshape(1, 1), bank_s,
         ],
         [
             pltpu.VMEM(cube, F32),
@@ -392,25 +544,21 @@
             pltpu.VMEM((TAPS * C, C), F32),
             pltpu.VMEM(cube, F32),
             pltpu.VMEM(cube, F32),
+            pltpu.VMEM(cube, F32),
+            pltpu.VMEM(cube, F32),
         ],
         flops=6_000_000_000,
         name="image",
+        limit=16,
     )
     got = lax.all_to_all(sent, "samp", 0, 0)
-    (features,) = call(
-        conv_kernel,
-        [((rows, cols, C), BF16)],
-        [low, block, high, taps],
-        flops=5_000_000_000,
-        name="conv",
-    )
-    shard = lax.axis_index("samp")
-    bank_s = lax.dynamic_slice_in_dim(bank, shard * width, width, 2).astype(F32)
+    got_other = lax.ppermute(got, "tok", swap)
     bank_grad, style_grad, select_grad = call(
         final_kernel,
-        [((NB, TAPS, width, C), F32), (style_weight.shape, F32), (select_weight.shape, F32)],
-        [got, bank_s],
+        [((NB, TAPS, width, C), F32), (style_weight.shape, F32), (select_weight.shape[::-1], F32)],
+        [got, got_other, bank_s],
         [
+            pltpu.VMEM((2, images, message, C), BF16),
             pltpu.VMEM((images, 16, C), F32),
             pltpu.VMEM((C, C), F32),
             pltpu.VMEM((images, TAPS, width, C), F32),
@@ -418,7 +566,7 @@
         ],
         name="final",
     )
-    return (features[None], penalty.reshape(1), bank_grad, style_grad, select_grad)
+    return (features[None], penalty.reshape(1), bank_grad, style_grad, select_grad.T)
 
 
 def solution(mesh):

time: 87.8 us -> 72.6 us (0.83)
  blocking collectives: 28.2 us -> 19.5 us
  local copies, waits for them, and re-layouts: 8.7 us -> 0.23 us
  waiting for transfers between devices: 13 us -> 6.29 us
  Pallas kernels: 17.8 us -> 22.5 us
  starting transfers between devices: 17.2 us -> 20.5 us
    ppermute x3 -> x11, starting transfers between devices: 6.61 us -> 17.3 us  [the longest x3 4.53 us: local(): came = [lax.ppermute(x, 'tok', along_y(j + 1)) for j, x in enumerate(out)]]
    all_to_all x2 -> x1, blocking collectives: 28.2 us -> 19.5 us  [local(): got = lax.all_to_all(sent, 'samp', 0, 0)]
    all_to_all x1 -> x0, starting transfers between devices: 8.32 us -> none  [local(): got = lax.all_to_all(sent, 'samp', 0, 0)]
    unnamed x20 -> x16, local copies, waits for them, and re-layouts: 7.69 us -> 0.23 us
    all_to_all x1 -> x0, waiting for transfers between devices: 7.04 us -> none  [local(): got = lax.all_to_all(sent, 'samp', 0, 0)]
    pallas_call x5 -> x12, Pallas kernels: 17.8 us -> 22.5 us  [the longest x9 15.4 us: call(): pl.pallas_call(kernel, out_shape=shapes, in_specs=specs, out_specs=whole(...]
    select_n x0 -> x1, other arithmetic: none -> 1.65 us  [neighbour_rows(): far = lax.ppermute(jnp.where(core == 0, first, last), 'tok', pairs)]
    slice x1 -> x0, local copies, waits for them, and re-layouts: 0.99 us -> none  [halo_rows(): high = lax.ppermute(block[:1], 'tok', backward)]
  transfers between devices with their start and end apart: 5 -> 12, of which waited for: 3 -> 6; matrix products, arithmetic and copies ran while one was open for 1% -> 0% of each run, Pallas kernels for 8% -> 21%
where the time goes in v2:
time: 72.6 us; the launch traced here: 72.1 us
  Pallas kernels  22.5 us (31%)
  starting transfers between devices  20.5 us (28%)
  blocking collectives  19.5 us (27%)
  waiting for transfers between devices  6.29 us (9%)
  other arithmetic  1.69 us (2%)
  between operations  1.49 us (2%)
    all_to_all x1, blocking collectives, local(): got = lax.all_to_all(sent, 'samp', 0, 0)  19.5 us
    pallas_call x9, Pallas kernels, call(): pl.pallas_call(kernel, out_shape=shapes, in_specs=specs, out_specs=whole(...  15.4 us
    pallas_call x3, Pallas kernels, conv_part(): pl.pallas_call(body, grid=(steps,), out_shape=[jax.ShapeDtypeStruct((rows...  7.05 us
    ppermute x3, starting transfers between devices, local(): came = [lax.ppermute(x, 'tok', along_y(j + 1)) for j, x in enumerate(out)]  4.53 us
    ppermute x3, starting transfers between devices, local(): came = [lax.ppermute(own, 'tok', along_y(j)) for j in (1, 2, 3)]  3.6 us
    ppermute x1, starting transfers between devices, neighbour_rows(): near = lax.ppermute(jnp.where(core == 0, last, first), 'tok', swap)  3.24 us
    ppermute x1, starting transfers between devices, local(): other = lax.ppermute(mine, 'tok', swap)  3.15 us
    ppermute x1, starting transfers between devices, local(): came = lax.ppermute(own, 'tok', [(i, i ^ 8) for i in range(toks)])  2.02 us
  transfers between devices with their start and end apart: 12, of which 6 were waited for; matrix products, arithmetic and copies ran while one was open for 0% of the time, Pallas kernels for 21%

profile of v2, /device:TPU:1, one launch (start us, length us, event | category | flops | bytes accessed | tf_op | source)
XLA Modules:
  0.0 72.1 jit_solution(12581785409623747326)
XLA Ops:
  0.6 1.6 %select_bitcast_fusion = (bf16[1,512,128]{2,1,0:T(8,128)(2,1)S(1)}, bf16[1,512,128]{2,1,0:T(8,128)(2,1)}) fusion(pred[]{:T(512)S(6)} %eq.6, bf16[1,16,512,128]{3,2,1,0:T(8,128)(2,1)} %param.7), kind=kLoop, calls=%fused_computation.1 | loop fusion | flops 131072 | bytes 524289 | tf_op jit(solution)/shard_map/jit(_where)/select_n | solution.py:459
  2.3 3.2 %collective-permute-start = (bf16[1,512,128]{2,1,0:T(8,128)(2,1)}, bf16[1,512,128]{2,1,0:T(8,128)(2,1)S(1)}, u32[]{:S(2)}, u32[]{:S(2)}) collective-permute-start(bf16[1,512,128]{2,1,0:T(8,128)(2,1)} %get-tuple-element.50), channel_id=1, source_target_pairs={{0,1},{1,0},{2,3},{3,2},{4,5},{5,4},{6,7},{7,6},{8,9},{9,8},{10,11... | collective-permute-start | bytes 393224 | tf_op jit(solution)/shard_map/ppermute | solution.py:460
  5.5 1.9 %collective-permute-start.1 = (bf16[1,512,128]{2,1,0:T(8,128)(2,1)S(1)}, bf16[1,512,128]{2,1,0:T(8,128)(2,1)S(1)}, u32[]{:S(2)}, u32[]{:S(2)}) collective-permute-start(bf16[1,512,128]{2,1,0:T(8,128)(2,1)S(1)} %get-tuple-element.49), channel_id=1, source_target_pairs={{1,2},{3,4},{5,6},{7,8},{9,10},{11,12},{13,14},{2,1},{4,3},{6,5},{... | collective-permute-start | bytes 393224 | tf_op jit(solution)/shard_map/ppermute | solution.py:459
  7.4 0.0 copy-start.1
  7.5 0.0 copy-start.2
  7.5 0.0 copy-start.3
  7.5 0.0 copy-start.4
  7.5 7.0 %corr.1 = (f32[1152,128]{1,0:T(8,128)}, bf16[384,512]{1,0:T(8,128)(2,1)}, bf16[384,512]{1,0:T(8,128)(2,1)}) custom-call(bf16[16,512,128]{2,1,0:T(8,128)(2,1)} %bitcast.12, bf16[16,512,128]{2,1,0:T(8,128)(2,1)} %bitcast.25), custom_call_target="tpu_custom_call" | custom-call | flops 4000000000 | bytes 4194304 | tf_op jit(solution)/shard_map/corr/pallas_call | solution.py:32
  14.5 0.0 copy-done.1
  14.6 0.0 copy-done.2
  14.6 0.0 copy-done.3
  14.6 0.0 copy-done.4
  14.6 0.0 copy-start.5
  14.6 0.0 copy-start.6
  14.6 0.0 copy-start.7
  14.6 1.0 %kernel_maker.1 = (bf16[512,768]{1,0:T(8,128)(2,1)S(1)}, f32[8,128]{1,0:T(8,128)S(1)}) custom-call(f32[1,512]{1,0:T(1,128)S(1)} %copy-done.4, bf16[8,9,128,128]{3,2,1,0:T(8,128)(2,1)S(1)} %copy-done.1, f32[512,128]{1,0:T(8,128)S(1)} %copy-done.2, f32[8,512]{1,0:T(8,128)S(1)} %bitcast.22), custom_call_target="tpu_custom_call" | custom-call | flops 2000000000 | bytes 2639872 | tf_op jit(solution)/shard_map/kernel_maker/pallas_call | solution.py:32
  15.6 0.0 copy-start
  15.7 0.0 collective-permute-done.near.refs_0_
  15.7 0.0 collective-permute-done.1.far.refs_1_
  15.7 0.1 copy-done.6
  15.8 0.1 copy-done.7
  15.9 0.5 edge.1
  16.4 0.1 collective-permute-start.2
  16.5 1.6 %collective-permute-done.2.given = f32[576,128]{1,0:T(8,128)S(1)} collective-permute-done((f32[576,128]{1,0:T(8,128)S(1)}, f32[576,128]{1,0:T(8,128)S(1)}, u32[]{:S(2)}, u32[]{:S(2)}) %collective-permute-start.2) | collective-permute-done | bytes 294944 | tf_op jit(solution)/shard_map/ppermute | solution.py:508
  18.1 1.6 %collective-permute-start.3 = (f32[144,128]{1,0:T(8,128)S(1)}, f32[144,128]{1,0:T(8,128)S(1)}, u32[]{:S(2)}, u32[]{:S(2)}) collective-permute-start(f32[144,128]{1,0:T(8,128)S(1)} %get-tuple-element.35), channel_id=1, source_target_pairs={{0,2},{1,3},{2,4},{3,5},{4,6},{5,7},{6,0},{7,1},{8,10},{9,11},{10,... | collective-permute-start | bytes 221192 | tf_op jit(solution)/shard_map/ppermute | solution.py:516
  19.7 3.0 %collective-permute-start.4 = (f32[144,128]{1,0:T(8,128)S(1)}, f32[144,128]{1,0:T(8,128)S(1)}, u32[]{:S(2)}, u32[]{:S(2)}) collective-permute-start(f32[144,128]{1,0:T(8,128)S(1)} %get-tuple-element.36), channel_id=1, source_target_pairs={{0,4},{1,5},{2,6},{3,7},{4,0},{5,1},{6,2},{7,3},{8,12},{9,13},{10,... | collective-permute-start | bytes 221192 | tf_op jit(solution)/shard_map/ppermute | solution.py:516
  22.7 0.0 collective-permute-start.5
  22.7 2.6 %conv.3 = (bf16[16,512,128]{2,1,0:T(8,128)(2,1)}, f32[8,128]{1,0:T(8,128)S(1)}) custom-call(bf16[1,512,128]{2,1,0:T(8,128)(2,1)S(1)} %collective-permute-done.near.refs_0_, bf16[1,512,128]{2,1,0:T(8,128)(2,1)S(1)} %collective-permute-done.1.far.refs_1_, bf16[16,512,128]{2,1,0:T(8,128)(2,1)S(1)} %bitcast.13, bf16[16,512,128]{2,1,0:T(8,128)(2,1)S(1)} %bitcast.14, ...), custom_call_target="tpu_custom_call" | custom-call | flops 1800000000 | bytes 2700000 | tf_op jit(solution)/shard_map/conv/pallas_call | solution.py:237
  25.3 0.0 collective-permute-done.3.refs_1_
  25.3 1.2 %collective-permute-done.4.refs_2_ = f32[144,128]{1,0:T(8,128)S(1)} collective-permute-done((f32[144,128]{1,0:T(8,128)S(1)}, f32[144,128]{1,0:T(8,128)S(1)}, u32[]{:S(2)}, u32[]{:S(2)}) %collective-permute-start.4) | collective-permute-done | bytes 73760 | tf_op jit(solution)/shard_map/ppermute | solution.py:516
  26.5 0.0 collective-permute-done.5.refs_3_
  26.5 2.0 %collective-permute-start.6 = (f32[144,128]{1,0:T(8,128)S(1)}, f32[144,128]{1,0:T(8,128)S(1)}, u32[]{:S(2)}, u32[]{:S(2)}) collective-permute-start(f32[144,128]{1,0:T(8,128)S(1)} %add_y.1.refs_6_.refs_0_), channel_id=1, source_target_pairs={{0,8},{1,9},{2,10},{3,11},{4,12},{5,13},{6,14},{7,15},{8,0},{9,1},... | collective-permute-start | bytes 221192 | tf_op jit(solution)/shard_map/ppermute | solution.py:519
  28.6 1.9 %conv.4 = (bf16[16,512,128]{2,1,0:T(8,128)(2,1)}, f32[8,128]{1,0:T(8,128)S(1)}) custom-call(bf16[1,512,128]{2,1,0:T(8,128)(2,1)S(1)} %collective-permute-done.near.refs_0_, bf16[1,512,128]{2,1,0:T(8,128)(2,1)S(1)} %collective-permute-done.1.far.refs_1_, bf16[16,512,128]{2,1,0:T(8,128)(2,1)S(1)} %bitcast.16, ...), custom_call_target="tpu_custom_call", output_to_operand_aliasing={{0}: (7, {})} | custom-call | flops 1200000000 | bytes 1800000 | tf_op jit(solution)/shard_map/conv/pallas_call | solution.py:237
  30.4 0.9 %collective-permute-done.6.refs_1_ = f32[144,128]{1,0:T(8,128)S(1)} collective-permute-done((f32[144,128]{1,0:T(8,128)S(1)}, f32[144,128]{1,0:T(8,128)S(1)}, u32[]{:S(2)}, u32[]{:S(2)}) %collective-permute-start.6) | collective-permute-done | bytes 73760 | tf_op jit(solution)/shard_map/ppermute | solution.py:519
  31.3 0.5 collective-permute-start.7
  31.8 3.1 %collective-permute-start.8 = (f32[144,128]{1,0:T(8,128)S(1)}, f32[144,128]{1,0:T(8,128)S(1)}, u32[]{:S(2)}, u32[]{:S(2)}) collective-permute-start(f32[144,128]{1,0:T(8,128)S(1)} %add_x.1.refs_6_.own), channel_id=1, source_target_pairs={{0,4},{1,5},{2,6},{3,7},{4,0},{5,1},{6,2},{7,3},{8,12},{9,13},{10,... | collective-permute-start | bytes 221192 | tf_op jit(solution)/shard_map/ppermute | solution.py:522
  34.9 0.0 collective-permute-start.9
  35.0 2.6 %conv.5 = (bf16[16,512,128]{2,1,0:T(8,128)(2,1)}, f32[8,128]{1,0:T(8,128)S(1)}) custom-call(bf16[1,512,128]{2,1,0:T(8,128)(2,1)S(1)} %collective-permute-done.near.refs_0_, bf16[1,512,128]{2,1,0:T(8,128)(2,1)S(1)} %collective-permute-done.1.far.refs_1_, bf16[16,512,128]{2,1,0:T(8,128)(2,1)S(1)} %bitcast.19, ...), custom_call_target="tpu_custom_call", output_to_operand_aliasing={{0}: (7, {})} | custom-call | flops 1800000000 | bytes 2700000 | tf_op jit(solution)/shard_map/conv/pallas_call | solution.py:237
  37.5 0.0 collective-permute-done.7.first
  37.5 0.0 collective-permute-done.8.second
  37.5 0.9 %collective-permute-done.9.third = f32[144,128]{1,0:T(8,128)S(1)} collective-permute-done((f32[144,128]{1,0:T(8,128)S(1)}, f32[144,128]{1,0:T(8,128)S(1)}, u32[]{:S(2)}, u32[]{:S(2)}) %collective-permute-start.9) | collective-permute-done | bytes 73760 | tf_op jit(solution)/shard_map/ppermute | solution.py:522
  38.5 3.1 %collective-permute-start.10 = (f32[576,128]{1,0:T(8,128)S(1)}, f32[576,128]{1,0:T(8,128)S(1)}, u32[]{:S(2)}, u32[]{:S(2)}) collective-permute-start(f32[576,128]{1,0:T(8,128)S(1)} %gather_y.1.refs_0_), channel_id=1, source_target_pairs={{0,1},{1,0},{2,3},{3,2},{4,5},{5,4},{6,7},{7,6},{8,9},{9,8},{10,11... | collective-permute-start | bytes 884744 | tf_op jit(solution)/shard_map/ppermute | solution.py:526
  42.3 0.5 collective-permute-done.10.refs_1_
  42.9 4.0 %image.1 = (bf16[16,64,128]{2,1,0:T(8,128)(2,1)S(1)}, f32[1,1]{1,0:T(1,128)}) custom-call(f32[576,128]{1,0:T(8,128)S(1)} %gather_y.1.refs_0_, f32[576,128]{1,0:T(8,128)S(1)} %collective-permute-done.10.refs_1_, f32[8,128]{1,0:T(8,128)S(1)} %get-tuple-element.31.rows.refs_2_, f32[1,512]{1,0:T(1,128)S(1)} %copy-done.4, bf16[8,9,128,128]{3,2,1,0:T(8,128)(2,1)S(1)} %copy-done.1, ...), custom_call_target="tpu_custom_call" | custom-call | flops 6000000000 | bytes 3528708 | tf_op jit(solution)/shard_map/image/pallas_call | solution.py:32
  46.8 19.5 %all_to_all.5.mine = bf16[16,64,128]{2,1,0:T(8,128)(2,1)S(1)} all-to-all(bf16[16,64,128]{2,1,0:T(8,128)(2,1)S(1)} %get-tuple-element.45), channel_id=1, replica_groups=mesh['samp'=16,'tok'=16] {'samp'}, dimensions={0} | all-to-all | bytes 524288 | tf_op jit(solution)/shard_map/all_to_all | solution.py:554
  66.3 1.9 %collective-permute-start.11 = (bf16[16,64,128]{2,1,0:T(8,128)(2,1)S(1)}, bf16[16,64,128]{2,1,0:T(8,128)(2,1)S(1)}, u32[]{:S(2)}, u32[]{:S(2)}) collective-permute-start(bf16[16,64,128]{2,1,0:T(8,128)(2,1)S(1)} %all_to_all.5.mine), channel_id=1, source_target_pairs={{0,1},{1,0},{2,3},{3,2},{4,5},{5,4},{6,7},{7,6},{8,9},{9,8},{10,11... | collective-permute-start | bytes 786440 | tf_op jit(solution)/shard_map/ppermute | solution.py:555
  68.3 1.2 %collective-permute-done.11.other = bf16[16,64,128]{2,1,0:T(8,128)(2,1)S(1)} collective-permute-done((bf16[16,64,128]{2,1,0:T(8,128)(2,1)S(1)}, bf16[16,64,128]{2,1,0:T(8,128)(2,1)S(1)}, u32[]{:S(2)}, u32[]{:S(2)}) %collective-permute-start.11) | collective-permute-done | bytes 262176 | tf_op jit(solution)/shard_map/ppermute | solution.py:555
  69.4 2.7 %final.1 = (f32[8,9,8,128]{3,2,1,0:T(8,128)}, f32[512,128]{1,0:T(8,128)}, f32[8,512]{1,0:T(8,128)}) custom-call(bf16[16,64,128]{2,1,0:T(8,128)(2,1)S(1)} %all_to_all.5.mine, bf16[16,64,128]{2,1,0:T(8,128)(2,1)S(1)} %collective-permute-done.11.other, f32[8,9,8,128]{3,2,1,0:T(8,128)S(1)} %dynamic-slice_convert_fusion.refs_8_.bank_s), custom_call_target="tpu_custom_call" | custom-call | bytes 819200 | tf_op jit(solution)/shard_map/final/pallas_call | solution.py:32
  (7 shorter events, 0.2 us)
Async XLA Ops:
  2.3 13.4 %collective-permute-start = (bf16[1,512,128]{2,1,0:T(8,128)(2,1)}, bf16[1,512,128]{2,1,0:T(8,128)(2,1)S(1)}, u32[]{:S(2)}, u32[]{:S(2)}) collective-permute-start(bf16[1,512,128]{2,1,0:T(8,128)(2,1)} %get-tuple-element.50), channel_id=1, source_target_pairs={{0,1},{1,0},{2,3},{3,2},{4,5},{5,4},{6,7},{7,6},{8,9},{9,8},{10,11... | collective-permute-start | bytes 393224 | tf_op jit(solution)/shard_map/ppermute | solution.py:460
  5.5 10.1 %collective-permute-start.1 = (bf16[1,512,128]{2,1,0:T(8,128)(2,1)S(1)}, bf16[1,512,128]{2,1,0:T(8,128)(2,1)S(1)}, u32[]{:S(2)}, u32[]{:S(2)}) collective-permute-start(bf16[1,512,128]{2,1,0:T(8,128)(2,1)S(1)} %get-tuple-element.49), channel_id=1, source_target_pairs={{1,2},{3,4},{5,6},{7,8},{9,10},{11,12},{13,14},{2,1},{4,3},{6,5},{... | collective-permute-start | bytes 393224 | tf_op jit(solution)/shard_map/ppermute | solution.py:459
  7.4 7.1 %copy-start.1 = (bf16[8,9,128,128]{3,2,1,0:T(8,128)(2,1)S(1)}, bf16[8,9,128,128]{3,2,1,0:T(8,128)(2,1)}, u32[]{:S(2)}) copy-start(bf16[8,9,128,128]{3,2,1,0:T(8,128)(2,1)} %refs_4_.1) | copy-start | bytes 7077892
  7.5 7.1 %copy-start.2 = (f32[512,128]{1,0:T(8,128)S(1)}, f32[512,128]{1,0:T(8,128)}, u32[]{:S(2)}) copy-start(f32[512,128]{1,0:T(8,128)} %refs_5_.1) | copy-start | bytes 786436
  7.5 7.1 %copy-start.3 = (f32[512,8]{0,1:T(8,128)S(1)}, f32[512,8]{0,1:T(8,128)}, u32[]{:S(2)}) copy-start(f32[512,8]{0,1:T(8,128)} %param.12) | copy-start | bytes 49156
  7.5 7.1 %copy-start.4 = (f32[1,512]{1,0:T(1,128)S(1)}, f32[1,512]{1,0:T(1,128)}, u32[]{:S(2)}) copy-start(f32[1,512]{1,0:T(1,128)} %refs_3_.1) | copy-start | bytes 6148
  14.6 1.1 %copy-start.5 = (f32[1152,128]{1,0:T(8,128)S(1)}, f32[1152,128]{1,0:T(8,128)}, u32[]{:S(2)}) copy-start(f32[1152,128]{1,0:T(8,128)} %get-tuple-element.28.flat) | copy-start | bytes 1769476
  14.6 1.2 %copy-start.6 = (bf16[384,512]{1,0:T(8,128)(2,1)S(1)}, bf16[384,512]{1,0:T(8,128)(2,1)}, u32[]{:S(2)}) copy-start(bf16[384,512]{1,0:T(8,128)(2,1)} %get-tuple-element.29.edge_low) | copy-start | bytes 1179652
  14.6 1.3 %copy-start.7 = (bf16[384,512]{1,0:T(8,128)(2,1)S(1)}, bf16[384,512]{1,0:T(8,128)(2,1)}, u32[]{:S(2)}) copy-start(bf16[384,512]{1,0:T(8,128)(2,1)} %get-tuple-element.30.edge_high) | copy-start | bytes 1179652
  15.6 7.0 %copy-start = (bf16[1,16,512,128]{3,2,1,0:T(8,128)(2,1)S(1)}, bf16[1,16,512,128]{3,2,1,0:T(8,128)(2,1)}, u32[]{:S(2)}) copy-start(bf16[1,16,512,128]{3,2,1,0:T(8,128)(2,1)} %param.7) | copy-start | bytes 6291460
  16.4 1.7 %collective-permute-start.2 = (f32[576,128]{1,0:T(8,128)S(1)}, f32[576,128]{1,0:T(8,128)S(1)}, u32[]{:S(2)}, u32[]{:S(2)}) collective-permute-start(f32[576,128]{1,0:T(8,128)S(1)} %get-tuple-element.33), channel_id=1, source_target_pairs={{0,1},{1,0},{2,3},{3,2},{4,5},{5,4},{6,7},{7,6},{8,9},{9,8},{10,11... | collective-permute-start | bytes 884744 | tf_op jit(solution)/shard_map/ppermute | solution.py:508
  18.1 7.1 %collective-permute-start.3 = (f32[144,128]{1,0:T(8,128)S(1)}, f32[144,128]{1,0:T(8,128)S(1)}, u32[]{:S(2)}, u32[]{:S(2)}) collective-permute-start(f32[144,128]{1,0:T(8,128)S(1)} %get-tuple-element.35), channel_id=1, source_target_pairs={{0,2},{1,3},{2,4},{3,5},{4,6},{5,7},{6,0},{7,1},{8,10},{9,11},{10,... | collective-permute-start | bytes 221192 | tf_op jit(solution)/shard_map/ppermute | solution.py:516
  19.7 6.8 %collective-permute-start.4 = (f32[144,128]{1,0:T(8,128)S(1)}, f32[144,128]{1,0:T(8,128)S(1)}, u32[]{:S(2)}, u32[]{:S(2)}) collective-permute-start(f32[144,128]{1,0:T(8,128)S(1)} %get-tuple-element.36), channel_id=1, source_target_pairs={{0,4},{1,5},{2,6},{3,7},{4,0},{5,1},{6,2},{7,3},{8,12},{9,13},{10,... | collective-permute-start | bytes 221192 | tf_op jit(solution)/shard_map/ppermute | solution.py:516
  22.7 3.8 %collective-permute-start.5 = (f32[144,128]{1,0:T(8,128)S(1)}, f32[144,128]{1,0:T(8,128)S(1)}, u32[]{:S(2)}, u32[]{:S(2)}) collective-permute-start(f32[144,128]{1,0:T(8,128)S(1)} %get-tuple-element.37), channel_id=1, source_target_pairs={{0,6},{1,7},{2,0},{3,1},{4,2},{5,3},{6,4},{7,5},{8,14},{9,15},{10,... | collective-permute-start | bytes 221192 | tf_op jit(solution)/shard_map/ppermute | solution.py:516
  26.5 4.8 %collective-permute-start.6 = (f32[144,128]{1,0:T(8,128)S(1)}, f32[144,128]{1,0:T(8,128)S(1)}, u32[]{:S(2)}, u32[]{:S(2)}) collective-permute-start(f32[144,128]{1,0:T(8,128)S(1)} %add_y.1.refs_6_.refs_0_), channel_id=1, source_target_pairs={{0,8},{1,9},{2,10},{3,11},{4,12},{5,13},{6,14},{7,15},{8,0},{9,1},... | collective-permute-start | bytes 221192 | tf_op jit(solution)/shard_map/ppermute | solution.py:519
  31.3 6.2 %collective-permute-start.7 = (f32[144,128]{1,0:T(8,128)S(1)}, f32[144,128]{1,0:T(8,128)S(1)}, u32[]{:S(2)}, u32[]{:S(2)}) collective-permute-start(f32[144,128]{1,0:T(8,128)S(1)} %add_x.1.refs_6_.own), channel_id=1, source_target_pairs={{0,2},{1,3},{2,4},{3,5},{4,6},{5,7},{6,0},{7,1},{8,10},{9,11},{10,... | collective-permute-start | bytes 221192 | tf_op jit(solution)/shard_map/ppermute | solution.py:522
  31.8 5.7 %collective-permute-start.8 = (f32[144,128]{1,0:T(8,128)S(1)}, f32[144,128]{1,0:T(8,128)S(1)}, u32[]{:S(2)}, u32[]{:S(2)}) collective-permute-start(f32[144,128]{1,0:T(8,128)S(1)} %add_x.1.refs_6_.own), channel_id=1, source_target_pairs={{0,4},{1,5},{2,6},{3,7},{4,0},{5,1},{6,2},{7,3},{8,12},{9,13},{10,... | collective-permute-start | bytes 221192 | tf_op jit(solution)/shard_map/ppermute | solution.py:522
  34.9 3.5 %collective-permute-start.9 = (f32[144,128]{1,0:T(8,128)S(1)}, f32[144,128]{1,0:T(8,128)S(1)}, u32[]{:S(2)}, u32[]{:S(2)}) collective-permute-start(f32[144,128]{1,0:T(8,128)S(1)} %add_x.1.refs_6_.own), channel_id=1, source_target_pairs={{0,6},{1,7},{2,0},{3,1},{4,2},{5,3},{6,4},{7,5},{8,14},{9,15},{10,... | collective-permute-start | bytes 221192 | tf_op jit(solution)/shard_map/ppermute | solution.py:522
  38.5 4.4 %collective-permute-start.10 = (f32[576,128]{1,0:T(8,128)S(1)}, f32[576,128]{1,0:T(8,128)S(1)}, u32[]{:S(2)}, u32[]{:S(2)}) collective-permute-start(f32[576,128]{1,0:T(8,128)S(1)} %gather_y.1.refs_0_), channel_id=1, source_target_pairs={{0,1},{1,0},{2,3},{3,2},{4,5},{5,4},{6,7},{7,6},{8,9},{9,8},{10,11... | collective-permute-start | bytes 884744 | tf_op jit(solution)/shard_map/ppermute | solution.py:526
  66.3 3.1 %collective-permute-start.11 = (bf16[16,64,128]{2,1,0:T(8,128)(2,1)S(1)}, bf16[16,64,128]{2,1,0:T(8,128)(2,1)S(1)}, u32[]{:S(2)}, u32[]{:S(2)}) collective-permute-start(bf16[16,64,128]{2,1,0:T(8,128)(2,1)S(1)} %all_to_all.5.mine), channel_id=1, source_target_pairs={{0,1},{1,0},{2,3},{3,2},{4,5},{5,4},{6,7},{7,6},{8,9},{9,8},{10,11... | collective-permute-start | bytes 786440 | tf_op jit(solution)/shard_map/ppermute | solution.py:555

commit v3 on v2

--- a/solution.py
+++ b/solution.py
@@ -15,7 +15,7 @@
 C = 128
 NB = 8
 GROUP = 4
-CORR_LIMIT = 61
+CORR_LIMIT = 51
 MIB = 1024 * 1024
 
 
@@ -172,7 +172,7 @@
             flat[tap * C : tap * C + C] = acc[kx * C : kx * C + C, ky * C : ky * C + C].T
 
 
-def edge_kernel(near, far, flat, edge_low, edge_high, rows, keep, give, both):
+def edge_kernel(near, far, flat, edge_low, edge_high, keep, give, both):
     core = lax.axis_index("tok") % 2
     first = jnp.where(core == 0, far[0], near[0])
     last = jnp.where(core == 0, near[0], far[0])
@@ -255,7 +255,7 @@
     )(*inputs)
 
 
-def split_kernel(keep, given, own, first, second, third):
+def split_kernel(keep, given, rows, own, first, second, third):
     place = lax.axis_index("tok") // 2 % 4
     size = own.shape[0]
     for step, out in enumerate((own, first, second, third)):
@@ -500,7 +500,7 @@
     keep, give = call(
         edge_kernel,
         [((half, C), F32)] * 2,
-        [near, far, flat, edge_low, edge_high, small],
+        [near, far, flat, edge_low, edge_high],
         [pltpu.VMEM((TAPS * C, C), F32)],
         flops=500_000_000,
         name="edge",
@@ -511,15 +511,16 @@
     def along_y(step):
         return [(i, i // 8 * 8 + (i + 2 * step) % 8) for i in range(toks)]
 
-    own, *out = call(split_kernel, [quarter] * 4, [keep, given], name="split")
+    own, *out = call(split_kernel, [quarter] * 4, [keep, given, small], name="split")
     features, token = conv_part(0, 3, near, far, block, taps, own, None)
-    came = [lax.ppermute(x, "tok", along_y(j + 1)) for j, x in enumerate(out)]
+    came = [lax.ppermute(out[j - 1], "tok", along_y(j)) for j in (2, 1, 3)]
     (own,) = call(add_kernel, [quarter], [own, *came, token], name="add_y")
     features, token = conv_part(3, 2, near, far, block, taps, own, features)
     came = lax.ppermute(own, "tok", [(i, i ^ 8) for i in range(toks)])
     (own,) = call(add_kernel, [quarter], [own, came, token], name="add_x")
     features, token = conv_part(5, 3, near, far, block, taps, own, features)
-    came = [lax.ppermute(own, "tok", along_y(j)) for j in (1, 2, 3)]
+    came = [lax.ppermute(own, "tok", along_y(j)) for j in (2, 1, 3)]
+    came = [came[1], came[0], came[2]]
     (mine,) = call(
         gather_kernel, [((half, C), F32)], [own, *came, token], name="gather_y"
     )

time: 72.6 us -> 70 us (0.964)
  waiting for transfers between devices: 6.29 us -> 2.3 us
  starting transfers between devices: 20.5 us -> 23.4 us
  Pallas kernels: 22.5 us -> 21.7 us
    ppermute x6, waiting for transfers between devices: 2.15 us -> 0.13 us  [the longest x3 0.12 us: local(): came = [lax.ppermute(out[j - 1], 'tok', along_y(j)) for j in (2, 1, 3)]]
    ppermute x1, starting transfers between devices: 2.02 us -> 3.29 us  [local(): came = lax.ppermute(own, 'tok', [(i, i ^ 8) for i in range(toks)])]
    ppermute x1, starting transfers between devices: 3.15 us -> 4.32 us  [local(): other = lax.ppermute(mine, 'tok', swap)]
    ppermute x1, waiting for transfers between devices: 1.57 us -> 0.49 us  [local(): given = lax.ppermute(give, 'tok', swap)]
    ppermute x1, waiting for transfers between devices: 0.9 us -> 0.01 us  [local(): came = lax.ppermute(own, 'tok', [(i, i ^ 8) for i in range(toks)])]
    pallas_call x9, Pallas kernels: 15.4 us -> 14.6 us  [call(): pl.pallas_call(kernel, out_shape=shapes, in_specs=specs, out_specs=whole(...]
  transfers between devices with their start and end apart: 12 -> 12, of which waited for: 6 -> 4; matrix products, arithmetic and copies ran while one was open for 0% -> 0% of each run, Pallas kernels for 21% -> 20%
where the time goes in v3:
time: 70 us; the launch traced here: 69.9 us
  starting transfers between devices  23.4 us (33%)
  Pallas kernels  21.7 us (31%)
  blocking collectives  20 us (29%)
  waiting for transfers between devices  2.3 us (3%)
  between operations  1.46 us (2%)
  other arithmetic  1.04 us (1%)
    all_to_all x1, blocking collectives, local(): got = lax.all_to_all(sent, 'samp', 0, 0)  20 us
    pallas_call x9, Pallas kernels, call(): pl.pallas_call(kernel, out_shape=shapes, in_specs=specs, out_specs=whole(...  14.6 us
    pallas_call x3, Pallas kernels, conv_part(): pl.pallas_call(body, grid=(steps,), out_shape=[jax.ShapeDtypeStruct((rows...  7.05 us
    ppermute x3, starting transfers between devices, local(): came = [lax.ppermute(out[j - 1], 'tok', along_y(j)) for j in (2, 1, 3)]  4.84 us
    ppermute x1, starting transfers between devices, local(): other = lax.ppermute(mine, 'tok', swap)  4.32 us
    ppermute x3, starting transfers between devices, local(): came = [lax.ppermute(own, 'tok', along_y(j)) for j in (2, 1, 3)]  3.69 us
    ppermute x1, starting transfers between devices, neighbour_rows(): near = lax.ppermute(jnp.where(core == 0, last, first), 'tok', swap)  3.33 us
    ppermute x1, starting transfers between devices, local(): came = lax.ppermute(own, 'tok', [(i, i ^ 8) for i in range(toks)])  3.29 us
  transfers between devices with their start and end apart: 12, of which 4 were waited for; matrix products, arithmetic and copies ran while one was open for 0% of the time, Pallas kernels for 20%

profile of v3, /device:TPU:1, one launch (start us, length us, event | category | flops | bytes accessed | tf_op | source)
XLA Modules:
  0.0 69.9 jit_solution(2159677303561427026)
XLA Ops:
  0.6 1.0 %select_bitcast_fusion = (bf16[1,512,128]{2,1,0:T(8,128)(2,1)S(1)}, bf16[1,512,128]{2,1,0:T(8,128)(2,1)S(1)}) fusion(pred[]{:T(512)S(6)} %eq.6, bf16[1,16,512,128]{3,2,1,0:T(8,128)(2,1)} %param.7), kind=kLoop, calls=%fused_computation.1 | loop fusion | flops 131072 | bytes 524289 | tf_op jit(solution)/shard_map/jit(_where)/select_n | solution.py:459
  1.6 3.3 %collective-permute-start = (bf16[1,512,128]{2,1,0:T(8,128)(2,1)S(1)}, bf16[1,512,128]{2,1,0:T(8,128)(2,1)S(1)}, u32[]{:S(2)}, u32[]{:S(2)}) collective-permute-start(bf16[1,512,128]{2,1,0:T(8,128)(2,1)S(1)} %get-tuple-element.50), channel_id=1, source_target_pairs={{0,1},{1,0},{2,3},{3,2},{4,5},{5,4},{6,7},{7,6},{8,9},{9,8},{10,11... | collective-permute-start | bytes 393224 | tf_op jit(solution)/shard_map/ppermute | solution.py:460
  5.0 1.9 %collective-permute-start.1 = (bf16[1,512,128]{2,1,0:T(8,128)(2,1)S(1)}, bf16[1,512,128]{2,1,0:T(8,128)(2,1)S(1)}, u32[]{:S(2)}, u32[]{:S(2)}) collective-permute-start(bf16[1,512,128]{2,1,0:T(8,128)(2,1)S(1)} %get-tuple-element.49), channel_id=1, source_target_pairs={{1,2},{3,4},{5,6},{7,8},{9,10},{11,12},{13,14},{2,1},{4,3},{6,5},{... | collective-permute-start | bytes 393224 | tf_op jit(solution)/shard_map/ppermute | solution.py:459
  6.9 0.0 copy-start.1
  6.9 0.0 copy-start.2
  6.9 0.0 copy-start.3
  6.9 0.0 copy-start.4
  6.9 6.2 %corr.1 = (f32[1152,128]{1,0:T(8,128)S(1)}, bf16[384,512]{1,0:T(8,128)(2,1)S(1)}, bf16[384,512]{1,0:T(8,128)(2,1)S(1)}) custom-call(bf16[16,512,128]{2,1,0:T(8,128)(2,1)} %bitcast.12, bf16[16,512,128]{2,1,0:T(8,128)(2,1)} %bitcast.25), custom_call_target="tpu_custom_call" | custom-call | flops 4000000000 | bytes 4194304 | tf_op jit(solution)/shard_map/corr/pallas_call | solution.py:32
  13.2 0.0 collective-permute-done.near.refs_0_
  13.2 0.0 collective-permute-done.1.far.refs_1_
  13.2 0.6 edge.1
  13.7 0.1 collective-permute-start.2
  13.8 0.0 copy-done.1
  13.9 0.0 copy-done.2
  13.9 0.0 copy-done.3
  13.9 0.0 copy-done.4
  13.9 0.0 copy-start
  13.9 1.0 %kernel_maker.1 = (bf16[512,768]{1,0:T(8,128)(2,1)S(1)}, f32[8,128]{1,0:T(8,128)S(1)}) custom-call(f32[1,512]{1,0:T(1,128)S(1)} %copy-done.4, bf16[8,9,128,128]{3,2,1,0:T(8,128)(2,1)S(1)} %copy-done.1, f32[512,128]{1,0:T(8,128)S(1)} %copy-done.2, f32[8,512]{1,0:T(8,128)S(1)} %bitcast.22), custom_call_target="tpu_custom_call" | custom-call | flops 2000000000 | bytes 2639872 | tf_op jit(solution)/shard_map/kernel_maker/pallas_call | solution.py:32
  14.9 0.5 collective-permute-done.2.given
  15.4 2.2 %collective-permute-start.3 = (f32[144,128]{1,0:T(8,128)S(1)}, f32[144,128]{1,0:T(8,128)S(1)}, u32[]{:S(2)}, u32[]{:S(2)}) collective-permute-start(f32[144,128]{1,0:T(8,128)S(1)} %get-tuple-element.35), channel_id=1, source_target_pairs={{0,4},{1,5},{2,6},{3,7},{4,0},{5,1},{6,2},{7,3},{8,12},{9,13},{10,... | collective-permute-start | bytes 221192 | tf_op jit(solution)/shard_map/ppermute | solution.py:516
  17.6 1.8 %collective-permute-start.4 = (f32[144,128]{1,0:T(8,128)S(1)}, f32[144,128]{1,0:T(8,128)S(1)}, u32[]{:S(2)}, u32[]{:S(2)}) collective-permute-start(f32[144,128]{1,0:T(8,128)S(1)} %get-tuple-element.36), channel_id=1, source_target_pairs={{0,2},{1,3},{2,4},{3,5},{4,6},{5,7},{6,0},{7,1},{8,10},{9,11},{10,... | collective-permute-start | bytes 221192 | tf_op jit(solution)/shard_map/ppermute | solution.py:516
  19.4 0.9 %collective-permute-start.5 = (f32[144,128]{1,0:T(8,128)S(1)}, f32[144,128]{1,0:T(8,128)S(1)}, u32[]{:S(2)}, u32[]{:S(2)}) collective-permute-start(f32[144,128]{1,0:T(8,128)S(1)} %get-tuple-element.37), channel_id=1, source_target_pairs={{0,6},{1,7},{2,0},{3,1},{4,2},{5,3},{6,4},{7,5},{8,14},{9,15},{10,... | collective-permute-start | bytes 221192 | tf_op jit(solution)/shard_map/ppermute | solution.py:516
  20.3 0.0 copy-done
  20.3 2.6 %conv.3 = (bf16[16,512,128]{2,1,0:T(8,128)(2,1)}, f32[8,128]{1,0:T(8,128)S(1)}) custom-call(bf16[1,512,128]{2,1,0:T(8,128)(2,1)S(1)} %collective-permute-done.near.refs_0_, bf16[1,512,128]{2,1,0:T(8,128)(2,1)S(1)} %collective-permute-done.1.far.refs_1_, bf16[16,512,128]{2,1,0:T(8,128)(2,1)S(1)} %bitcast.13, bf16[16,512,128]{2,1,0:T(8,128)(2,1)S(1)} %bitcast.14, ...), custom_call_target="tpu_custom_call" | custom-call | flops 1800000000 | bytes 2700000 | tf_op jit(solution)/shard_map/conv/pallas_call | solution.py:237
  22.9 0.0 collective-permute-done.3.refs_1_
  22.9 0.0 collective-permute-done.4.refs_2_
  22.9 0.1 collective-permute-done.5.refs_3_
  23.0 3.3 %collective-permute-start.6 = (f32[144,128]{1,0:T(8,128)S(1)}, f32[144,128]{1,0:T(8,128)S(1)}, u32[]{:S(2)}, u32[]{:S(2)}) collective-permute-start(f32[144,128]{1,0:T(8,128)S(1)} %add_y.1.refs_6_.refs_0_), channel_id=1, source_target_pairs={{0,8},{1,9},{2,10},{3,11},{4,12},{5,13},{6,14},{7,15},{8,0},{9,1},... | collective-permute-start | bytes 221192 | tf_op jit(solution)/shard_map/ppermute | solution.py:519
  26.3 1.9 %conv.4 = (bf16[16,512,128]{2,1,0:T(8,128)(2,1)}, f32[8,128]{1,0:T(8,128)S(1)}) custom-call(bf16[1,512,128]{2,1,0:T(8,128)(2,1)S(1)} %collective-permute-done.near.refs_0_, bf16[1,512,128]{2,1,0:T(8,128)(2,1)S(1)} %collective-permute-done.1.far.refs_1_, bf16[16,512,128]{2,1,0:T(8,128)(2,1)S(1)} %bitcast.16, ...), custom_call_target="tpu_custom_call", output_to_operand_aliasing={{0}: (7, {})} | custom-call | flops 1200000000 | bytes 1800000 | tf_op jit(solution)/shard_map/conv/pallas_call | solution.py:237
  28.2 0.0 collective-permute-done.6.refs_1_
  28.2 0.9 %collective-permute-start.7 = (f32[144,128]{1,0:T(8,128)S(1)}, f32[144,128]{1,0:T(8,128)S(1)}, u32[]{:S(2)}, u32[]{:S(2)}) collective-permute-start(f32[144,128]{1,0:T(8,128)S(1)} %add_x.1.refs_6_.own), channel_id=1, source_target_pairs={{0,2},{1,3},{2,4},{3,5},{4,6},{5,7},{6,0},{7,1},{8,10},{9,11},{10,... | collective-permute-start | bytes 221192 | tf_op jit(solution)/shard_map/ppermute | solution.py:522
  29.2 2.0 %collective-permute-start.8 = (f32[144,128]{1,0:T(8,128)S(1)}, f32[144,128]{1,0:T(8,128)S(1)}, u32[]{:S(2)}, u32[]{:S(2)}) collective-permute-start(f32[144,128]{1,0:T(8,128)S(1)} %add_x.1.refs_6_.own), channel_id=1, source_target_pairs={{0,4},{1,5},{2,6},{3,7},{4,0},{5,1},{6,2},{7,3},{8,12},{9,13},{10,... | collective-permute-start | bytes 221192 | tf_op jit(solution)/shard_map/ppermute | solution.py:522
  31.2 0.7 %collective-permute-start.9 = (f32[144,128]{1,0:T(8,128)S(1)}, f32[144,128]{1,0:T(8,128)S(1)}, u32[]{:S(2)}, u32[]{:S(2)}) collective-permute-start(f32[144,128]{1,0:T(8,128)S(1)} %add_x.1.refs_6_.own), channel_id=1, source_target_pairs={{0,6},{1,7},{2,0},{3,1},{4,2},{5,3},{6,4},{7,5},{8,14},{9,15},{10,... | collective-permute-start | bytes 221192 | tf_op jit(solution)/shard_map/ppermute | solution.py:522
  31.9 2.6 %conv.5 = (bf16[16,512,128]{2,1,0:T(8,128)(2,1)}, f32[8,128]{1,0:T(8,128)S(1)}) custom-call(bf16[1,512,128]{2,1,0:T(8,128)(2,1)S(1)} %collective-permute-done.near.refs_0_, bf16[1,512,128]{2,1,0:T(8,128)(2,1)S(1)} %collective-permute-done.1.far.refs_1_, bf16[16,512,128]{2,1,0:T(8,128)(2,1)S(1)} %bitcast.19, ...), custom_call_target="tpu_custom_call", output_to_operand_aliasing={{0}: (7, {})} | custom-call | flops 1800000000 | bytes 2700000 | tf_op jit(solution)/shard_map/conv/pallas_call | solution.py:237
  34.5 0.0 collective-permute-done.7.first
  34.5 0.0 collective-permute-done.8.second
  34.5 0.0 collective-permute-done.9.third
  34.6 4.3 %collective-permute-start.10 = (f32[576,128]{1,0:T(8,128)S(1)}, f32[576,128]{1,0:T(8,128)S(1)}, u32[]{:S(2)}, u32[]{:S(2)}) collective-permute-start(f32[576,128]{1,0:T(8,128)S(1)} %gather_y.1.refs_0_), channel_id=1, source_target_pairs={{0,1},{1,0},{2,3},{3,2},{4,5},{5,4},{6,7},{7,6},{8,9},{9,8},{10,11... | collective-permute-start | bytes 884744 | tf_op jit(solution)/shard_map/ppermute | solution.py:527
  39.6 0.5 collective-permute-done.10.refs_1_
  40.1 4.0 %image.1 = (bf16[16,64,128]{2,1,0:T(8,128)(2,1)S(1)}, f32[1,1]{1,0:T(1,128)}) custom-call(f32[576,128]{1,0:T(8,128)S(1)} %gather_y.1.refs_0_, f32[576,128]{1,0:T(8,128)S(1)} %collective-permute-done.10.refs_1_, f32[8,128]{1,0:T(8,128)S(1)} %get-tuple-element.33.rows.refs_2_, f32[1,512]{1,0:T(1,128)S(1)} %copy-done.4, bf16[8,9,128,128]{3,2,1,0:T(8,128)(2,1)S(1)} %copy-done.1, ...), custom_call_target="tpu_custom_call" | custom-call | flops 6000000000 | bytes 3528708 | tf_op jit(solution)/shard_map/image/pallas_call | solution.py:32
  44.1 20.0 %all_to_all.5.mine = bf16[16,64,128]{2,1,0:T(8,128)(2,1)S(1)} all-to-all(bf16[16,64,128]{2,1,0:T(8,128)(2,1)S(1)} %get-tuple-element.45), channel_id=1, replica_groups=mesh['samp'=16,'tok'=16] {'samp'}, dimensions={0} | all-to-all | bytes 524288 | tf_op jit(solution)/shard_map/all_to_all | solution.py:555
  64.1 1.9 %collective-permute-start.11 = (bf16[16,64,128]{2,1,0:T(8,128)(2,1)S(1)}, bf16[16,64,128]{2,1,0:T(8,128)(2,1)S(1)}, u32[]{:S(2)}, u32[]{:S(2)}) collective-permute-start(bf16[16,64,128]{2,1,0:T(8,128)(2,1)S(1)} %all_to_all.5.mine), channel_id=1, source_target_pairs={{0,1},{1,0},{2,3},{3,2},{4,5},{5,4},{6,7},{7,6},{8,9},{9,8},{10,11... | collective-permute-start | bytes 786440 | tf_op jit(solution)/shard_map/ppermute | solution.py:556
  66.0 1.2 %collective-permute-done.11.other = bf16[16,64,128]{2,1,0:T(8,128)(2,1)S(1)} collective-permute-done((bf16[16,64,128]{2,1,0:T(8,128)(2,1)S(1)}, bf16[16,64,128]{2,1,0:T(8,128)(2,1)S(1)}, u32[]{:S(2)}, u32[]{:S(2)}) %collective-permute-start.11) | collective-permute-done | bytes 262176 | tf_op jit(solution)/shard_map/ppermute | solution.py:556
  67.2 2.7 %final.1 = (f32[8,9,8,128]{3,2,1,0:T(8,128)}, f32[512,128]{1,0:T(8,128)}, f32[8,512]{1,0:T(8,128)}) custom-call(bf16[16,64,128]{2,1,0:T(8,128)(2,1)S(1)} %all_to_all.5.mine, bf16[16,64,128]{2,1,0:T(8,128)(2,1)S(1)} %collective-permute-done.11.other, f32[8,9,8,128]{3,2,1,0:T(8,128)S(1)} %dynamic-slice_convert_fusion.refs_8_.bank_s), custom_call_target="tpu_custom_call" | custom-call | bytes 819200 | tf_op jit(solution)/shard_map/final/pallas_call | solution.py:32
  (5 shorter events, 0.2 us)
Async XLA Ops:
  1.6 11.5 %collective-permute-start = (bf16[1,512,128]{2,1,0:T(8,128)(2,1)S(1)}, bf16[1,512,128]{2,1,0:T(8,128)(2,1)S(1)}, u32[]{:S(2)}, u32[]{:S(2)}) collective-permute-start(bf16[1,512,128]{2,1,0:T(8,128)(2,1)S(1)} %get-tuple-element.50), channel_id=1, source_target_pairs={{0,1},{1,0},{2,3},{3,2},{4,5},{5,4},{6,7},{7,6},{8,9},{9,8},{10,11... | collective-permute-start | bytes 393224 | tf_op jit(solution)/shard_map/ppermute | solution.py:460
  5.0 8.2 %collective-permute-start.1 = (bf16[1,512,128]{2,1,0:T(8,128)(2,1)S(1)}, bf16[1,512,128]{2,1,0:T(8,128)(2,1)S(1)}, u32[]{:S(2)}, u32[]{:S(2)}) collective-permute-start(bf16[1,512,128]{2,1,0:T(8,128)(2,1)S(1)} %get-tuple-element.49), channel_id=1, source_target_pairs={{1,2},{3,4},{5,6},{7,8},{9,10},{11,12},{13,14},{2,1},{4,3},{6,5},{... | collective-permute-start | bytes 393224 | tf_op jit(solution)/shard_map/ppermute | solution.py:459
  6.9 7.0 %copy-start.1 = (bf16[8,9,128,128]{3,2,1,0:T(8,128)(2,1)S(1)}, bf16[8,9,128,128]{3,2,1,0:T(8,128)(2,1)}, u32[]{:S(2)}) copy-start(bf16[8,9,128,128]{3,2,1,0:T(8,128)(2,1)} %refs_4_.1) | copy-start | bytes 7077892
  6.9 7.0 %copy-start.2 = (f32[512,128]{1,0:T(8,128)S(1)}, f32[512,128]{1,0:T(8,128)}, u32[]{:S(2)}) copy-start(f32[512,128]{1,0:T(8,128)} %refs_5_.1) | copy-start | bytes 786436
  6.9 7.0 %copy-start.3 = (f32[512,8]{0,1:T(8,128)S(1)}, f32[512,8]{0,1:T(8,128)}, u32[]{:S(2)}) copy-start(f32[512,8]{0,1:T(8,128)} %param.12) | copy-start | bytes 49156
  6.9 7.0 %copy-start.4 = (f32[1,512]{1,0:T(1,128)S(1)}, f32[1,512]{1,0:T(1,128)}, u32[]{:S(2)}) copy-start(f32[1,512]{1,0:T(1,128)} %refs_3_.1) | copy-start | bytes 6148
  13.7 1.7 %collective-permute-start.2 = (f32[576,128]{1,0:T(8,128)S(1)}, f32[576,128]{1,0:T(8,128)S(1)}, u32[]{:S(2)}, u32[]{:S(2)}) collective-permute-start(f32[576,128]{1,0:T(8,128)S(1)} %get-tuple-element.32), channel_id=1, source_target_pairs={{0,1},{1,0},{2,3},{3,2},{4,5},{5,4},{6,7},{7,6},{8,9},{9,8},{10,11... | collective-permute-start | bytes 884744 | tf_op jit(solution)/shard_map/ppermute | solution.py:508
  13.9 6.4 %copy-start = (bf16[1,16,512,128]{3,2,1,0:T(8,128)(2,1)S(1)}, bf16[1,16,512,128]{3,2,1,0:T(8,128)(2,1)}, u32[]{:S(2)}) copy-start(bf16[1,16,512,128]{3,2,1,0:T(8,128)(2,1)} %param.7) | copy-start | bytes 6291460
  15.4 7.4 %collective-permute-start.3 = (f32[144,128]{1,0:T(8,128)S(1)}, f32[144,128]{1,0:T(8,128)S(1)}, u32[]{:S(2)}, u32[]{:S(2)}) collective-permute-start(f32[144,128]{1,0:T(8,128)S(1)} %get-tuple-element.35), channel_id=1, source_target_pairs={{0,4},{1,5},{2,6},{3,7},{4,0},{5,1},{6,2},{7,3},{8,12},{9,13},{10,... | collective-permute-start | bytes 221192 | tf_op jit(solution)/shard_map/ppermute | solution.py:516
  17.6 5.3 %collective-permute-start.4 = (f32[144,128]{1,0:T(8,128)S(1)}, f32[144,128]{1,0:T(8,128)S(1)}, u32[]{:S(2)}, u32[]{:S(2)}) collective-permute-start(f32[144,128]{1,0:T(8,128)S(1)} %get-tuple-element.36), channel_id=1, source_target_pairs={{0,2},{1,3},{2,4},{3,5},{4,6},{5,7},{6,0},{7,1},{8,10},{9,11},{10,... | collective-permute-start | bytes 221192 | tf_op jit(solution)/shard_map/ppermute | solution.py:516
  19.4 3.6 %collective-permute-start.5 = (f32[144,128]{1,0:T(8,128)S(1)}, f32[144,128]{1,0:T(8,128)S(1)}, u32[]{:S(2)}, u32[]{:S(2)}) collective-permute-start(f32[144,128]{1,0:T(8,128)S(1)} %get-tuple-element.37), channel_id=1, source_target_pairs={{0,6},{1,7},{2,0},{3,1},{4,2},{5,3},{6,4},{7,5},{8,14},{9,15},{10,... | collective-permute-start | bytes 221192 | tf_op jit(solution)/shard_map/ppermute | solution.py:516
  23.0 5.2 %collective-permute-start.6 = (f32[144,128]{1,0:T(8,128)S(1)}, f32[144,128]{1,0:T(8,128)S(1)}, u32[]{:S(2)}, u32[]{:S(2)}) collective-permute-start(f32[144,128]{1,0:T(8,128)S(1)} %add_y.1.refs_6_.refs_0_), channel_id=1, source_target_pairs={{0,8},{1,9},{2,10},{3,11},{4,12},{5,13},{6,14},{7,15},{8,0},{9,1},... | collective-permute-start | bytes 221192 | tf_op jit(solution)/shard_map/ppermute | solution.py:519
  28.2 6.3 %collective-permute-start.7 = (f32[144,128]{1,0:T(8,128)S(1)}, f32[144,128]{1,0:T(8,128)S(1)}, u32[]{:S(2)}, u32[]{:S(2)}) collective-permute-start(f32[144,128]{1,0:T(8,128)S(1)} %add_x.1.refs_6_.own), channel_id=1, source_target_pairs={{0,2},{1,3},{2,4},{3,5},{4,6},{5,7},{6,0},{7,1},{8,10},{9,11},{10,... | collective-permute-start | bytes 221192 | tf_op jit(solution)/shard_map/ppermute | solution.py:522
  29.2 5.3 %collective-permute-start.8 = (f32[144,128]{1,0:T(8,128)S(1)}, f32[144,128]{1,0:T(8,128)S(1)}, u32[]{:S(2)}, u32[]{:S(2)}) collective-permute-start(f32[144,128]{1,0:T(8,128)S(1)} %add_x.1.refs_6_.own), channel_id=1, source_target_pairs={{0,4},{1,5},{2,6},{3,7},{4,0},{5,1},{6,2},{7,3},{8,12},{9,13},{10,... | collective-permute-start | bytes 221192 | tf_op jit(solution)/shard_map/ppermute | solution.py:522
  31.2 3.3 %collective-permute-start.9 = (f32[144,128]{1,0:T(8,128)S(1)}, f32[144,128]{1,0:T(8,128)S(1)}, u32[]{:S(2)}, u32[]{:S(2)}) collective-permute-start(f32[144,128]{1,0:T(8,128)S(1)} %add_x.1.refs_6_.own), channel_id=1, source_target_pairs={{0,6},{1,7},{2,0},{3,1},{4,2},{5,3},{6,4},{7,5},{8,14},{9,15},{10,... | collective-permute-start | bytes 221192 | tf_op jit(solution)/shard_map/ppermute | solution.py:522
  34.6 5.5 %collective-permute-start.10 = (f32[576,128]{1,0:T(8,128)S(1)}, f32[576,128]{1,0:T(8,128)S(1)}, u32[]{:S(2)}, u32[]{:S(2)}) collective-permute-start(f32[576,128]{1,0:T(8,128)S(1)} %gather_y.1.refs_0_), channel_id=1, source_target_pairs={{0,1},{1,0},{2,3},{3,2},{4,5},{5,4},{6,7},{7,6},{8,9},{9,8},{10,11... | collective-permute-start | bytes 884744 | tf_op jit(solution)/shard_map/ppermute | solution.py:527
  64.1 3.1 %collective-permute-start.11 = (bf16[16,64,128]{2,1,0:T(8,128)(2,1)S(1)}, bf16[16,64,128]{2,1,0:T(8,128)(2,1)S(1)}, u32[]{:S(2)}, u32[]{:S(2)}) collective-permute-start(bf16[16,64,128]{2,1,0:T(8,128)(2,1)S(1)} %all_to_all.5.mine), channel_id=1, source_target_pairs={{0,1},{1,0},{2,3},{3,2},{4,5},{5,4},{6,7},{7,6},{8,9},{9,8},{10,11... | collective-permute-start | bytes 786440 | tf_op jit(solution)/shard_map/ppermute | solution.py:556

commit v4 on v3

--- a/solution.py
+++ b/solution.py
@@ -14,7 +14,7 @@
 TAPS = 9
 C = 128
 NB = 8
-GROUP = 4
+GROUP = 8
 CORR_LIMIT = 51
 MIB = 1024 * 1024
 
@@ -293,11 +293,9 @@
 ):
     core = lax.axis_index("tok") % 2
     half = TAPS * C // 2
-    terms_flat = terms
-    terms_flat[pl.ds(pl.multiple_of(core * half, 8), half)] = mine[...] * scale
-    terms_flat[pl.ds(pl.multiple_of((1 - core) * half, 8), half)] = other[...] * scale
-    for tap in range(TAPS):
-        corr[tap] = terms_flat[tap * C : tap * C + C]
+    flat = corr.reshape(TAPS * C, C)
+    flat[pl.ds(pl.multiple_of(core * half, 8), half)] = mine[...] * scale
+    flat[pl.ds(pl.multiple_of((1 - core) * half, 8), half)] = other[...] * scale
     style, demod, share = rows[0:1], rows[1:2], rows[2:3]
     style_d = down(style)
     demod3 = demod * demod * demod

time: 70 us -> 70.1 us (level)
  transfers between devices with their start and end apart: 12 -> 12, of which waited for: 4 -> 5; matrix products, arithmetic and copies ran while one was open for 0% -> 0% of each run, Pallas kernels for 20% -> 20%
where the time goes in v4:
time: 70.1 us; the launch traced here: 70 us
  starting transfers between devices  23.1 us (33%)
  Pallas kernels  21.5 us (31%)
  blocking collectives  20 us (29%)
  waiting for transfers between devices  2.82 us (4%)
  between operations  1.46 us (2%)
  other arithmetic  1.04 us (1%)
    all_to_all x1, blocking collectives, local(): got = lax.all_to_all(sent, 'samp', 0, 0)  20 us
    pallas_call x9, Pallas kernels, call(): pl.pallas_call(kernel, out_shape=shapes, in_specs=specs, out_specs=whole(...  14.5 us
    pallas_call x3, Pallas kernels, conv_part(): pl.pallas_call(body, grid=(steps,), out_shape=[jax.ShapeDtypeStruct((rows...  7.05 us
    ppermute x3, starting transfers between devices, local(): came = [lax.ppermute(out[j - 1], 'tok', along_y(j)) for j in (2, 1, 3)]  4.85 us
    ppermute x1, starting transfers between devices, local(): other = lax.ppermute(mine, 'tok', swap)  4.01 us
    ppermute x3, starting transfers between devices, local(): came = [lax.ppermute(own, 'tok', along_y(j)) for j in (2, 1, 3)]  3.68 us
    ppermute x1, starting transfers between devices, neighbour_rows(): near = lax.ppermute(jnp.where(core == 0, last, first), 'tok', swap)  3.33 us
    ppermute x1, starting transfers between devices, local(): came = lax.ppermute(own, 'tok', [(i, i ^ 8) for i in range(toks)])  3.3 us
  transfers between devices with their start and end apart: 12, of which 5 were waited for; matrix products, arithmetic and copies ran while one was open for 0% of the time, Pallas kernels for 20%

profile of v4, /device:TPU:1, one launch (start us, length us, event | category | flops | bytes accessed | tf_op | source)
XLA Modules:
  0.0 70.0 jit_solution(2262432014653326815)
XLA Ops:
  0.6 1.0 %select_bitcast_fusion = (bf16[1,512,128]{2,1,0:T(8,128)(2,1)S(1)}, bf16[1,512,128]{2,1,0:T(8,128)(2,1)S(1)}) fusion(pred[]{:T(512)S(6)} %eq.6, bf16[1,16,512,128]{3,2,1,0:T(8,128)(2,1)} %param.7), kind=kLoop, calls=%fused_computation.1 | loop fusion | flops 131072 | bytes 524289 | tf_op jit(solution)/shard_map/jit(_where)/select_n | solution.py:457
  1.6 3.3 %collective-permute-start = (bf16[1,512,128]{2,1,0:T(8,128)(2,1)S(1)}, bf16[1,512,128]{2,1,0:T(8,128)(2,1)S(1)}, u32[]{:S(2)}, u32[]{:S(2)}) collective-permute-start(bf16[1,512,128]{2,1,0:T(8,128)(2,1)S(1)} %get-tuple-element.50), channel_id=1, source_target_pairs={{0,1},{1,0},{2,3},{3,2},{4,5},{5,4},{6,7},{7,6},{8,9},{9,8},{10,11... | collective-permute-start | bytes 393224 | tf_op jit(solution)/shard_map/ppermute | solution.py:458
  5.0 1.9 %collective-permute-start.1 = (bf16[1,512,128]{2,1,0:T(8,128)(2,1)S(1)}, bf16[1,512,128]{2,1,0:T(8,128)(2,1)S(1)}, u32[]{:S(2)}, u32[]{:S(2)}) collective-permute-start(bf16[1,512,128]{2,1,0:T(8,128)(2,1)S(1)} %get-tuple-element.49), channel_id=1, source_target_pairs={{1,2},{3,4},{5,6},{7,8},{9,10},{11,12},{13,14},{2,1},{4,3},{6,5},{... | collective-permute-start | bytes 393224 | tf_op jit(solution)/shard_map/ppermute | solution.py:457
  6.9 0.0 copy-start.1
  6.9 0.0 copy-start.2
  6.9 0.0 copy-start.3
  6.9 0.0 copy-start.4
  6.9 6.1 %corr.1 = (f32[1152,128]{1,0:T(8,128)S(1)}, bf16[384,512]{1,0:T(8,128)(2,1)S(1)}, bf16[384,512]{1,0:T(8,128)(2,1)S(1)}) custom-call(bf16[16,512,128]{2,1,0:T(8,128)(2,1)} %bitcast.12, bf16[16,512,128]{2,1,0:T(8,128)(2,1)} %bitcast.25), custom_call_target="tpu_custom_call" | custom-call | flops 4000000000 | bytes 4194304 | tf_op jit(solution)/shard_map/corr/pallas_call | solution.py:32
  13.0 0.0 collective-permute-done.near.refs_0_
  13.0 0.0 collective-permute-done.1.far.refs_1_
  13.1 0.6 edge.1
  13.6 0.1 collective-permute-start.2
  13.7 0.0 copy-done.1
  13.7 0.0 copy-done.2
  13.7 0.0 copy-done.3
  13.8 0.0 copy-done.4
  13.8 0.0 copy-start
  13.8 1.0 %kernel_maker.1 = (bf16[512,768]{1,0:T(8,128)(2,1)S(1)}, f32[8,128]{1,0:T(8,128)S(1)}) custom-call(f32[1,512]{1,0:T(1,128)S(1)} %copy-done.4, bf16[8,9,128,128]{3,2,1,0:T(8,128)(2,1)S(1)} %copy-done.1, f32[512,128]{1,0:T(8,128)S(1)} %copy-done.2, f32[8,512]{1,0:T(8,128)S(1)} %bitcast.22), custom_call_target="tpu_custom_call" | custom-call | flops 2000000000 | bytes 2639872 | tf_op jit(solution)/shard_map/kernel_maker/pallas_call | solution.py:32
  14.8 0.5 collective-permute-done.2.given
  15.3 2.2 %collective-permute-start.3 = (f32[144,128]{1,0:T(8,128)S(1)}, f32[144,128]{1,0:T(8,128)S(1)}, u32[]{:S(2)}, u32[]{:S(2)}) collective-permute-start(f32[144,128]{1,0:T(8,128)S(1)} %get-tuple-element.35), channel_id=1, source_target_pairs={{0,4},{1,5},{2,6},{3,7},{4,0},{5,1},{6,2},{7,3},{8,12},{9,13},{10,... | collective-permute-start | bytes 221192 | tf_op jit(solution)/shard_map/ppermute | solution.py:514
  17.5 1.8 %collective-permute-start.4 = (f32[144,128]{1,0:T(8,128)S(1)}, f32[144,128]{1,0:T(8,128)S(1)}, u32[]{:S(2)}, u32[]{:S(2)}) collective-permute-start(f32[144,128]{1,0:T(8,128)S(1)} %get-tuple-element.36), channel_id=1, source_target_pairs={{0,2},{1,3},{2,4},{3,5},{4,6},{5,7},{6,0},{7,1},{8,10},{9,11},{10,... | collective-permute-start | bytes 221192 | tf_op jit(solution)/shard_map/ppermute | solution.py:514
  19.3 0.9 %collective-permute-start.5 = (f32[144,128]{1,0:T(8,128)S(1)}, f32[144,128]{1,0:T(8,128)S(1)}, u32[]{:S(2)}, u32[]{:S(2)}) collective-permute-start(f32[144,128]{1,0:T(8,128)S(1)} %get-tuple-element.37), channel_id=1, source_target_pairs={{0,6},{1,7},{2,0},{3,1},{4,2},{5,3},{6,4},{7,5},{8,14},{9,15},{10,... | collective-permute-start | bytes 221192 | tf_op jit(solution)/shard_map/ppermute | solution.py:514
  20.2 0.0 copy-done
  20.2 2.6 %conv.3 = (bf16[16,512,128]{2,1,0:T(8,128)(2,1)}, f32[8,128]{1,0:T(8,128)S(1)}) custom-call(bf16[1,512,128]{2,1,0:T(8,128)(2,1)S(1)} %collective-permute-done.near.refs_0_, bf16[1,512,128]{2,1,0:T(8,128)(2,1)S(1)} %collective-permute-done.1.far.refs_1_, bf16[16,512,128]{2,1,0:T(8,128)(2,1)S(1)} %bitcast.13, bf16[16,512,128]{2,1,0:T(8,128)(2,1)S(1)} %bitcast.14, ...), custom_call_target="tpu_custom_call" | custom-call | flops 1800000000 | bytes 2700000 | tf_op jit(solution)/shard_map/conv/pallas_call | solution.py:237
  22.8 0.0 collective-permute-done.3.refs_1_
  22.8 0.0 collective-permute-done.4.refs_2_
  22.8 0.1 collective-permute-done.5.refs_3_
  22.9 3.3 %collective-permute-start.6 = (f32[144,128]{1,0:T(8,128)S(1)}, f32[144,128]{1,0:T(8,128)S(1)}, u32[]{:S(2)}, u32[]{:S(2)}) collective-permute-start(f32[144,128]{1,0:T(8,128)S(1)} %add_y.1.refs_6_.refs_0_), channel_id=1, source_target_pairs={{0,8},{1,9},{2,10},{3,11},{4,12},{5,13},{6,14},{7,15},{8,0},{9,1},... | collective-permute-start | bytes 221192 | tf_op jit(solution)/shard_map/ppermute | solution.py:517
  26.2 1.9 %conv.4 = (bf16[16,512,128]{2,1,0:T(8,128)(2,1)}, f32[8,128]{1,0:T(8,128)S(1)}) custom-call(bf16[1,512,128]{2,1,0:T(8,128)(2,1)S(1)} %collective-permute-done.near.refs_0_, bf16[1,512,128]{2,1,0:T(8,128)(2,1)S(1)} %collective-permute-done.1.far.refs_1_, bf16[16,512,128]{2,1,0:T(8,128)(2,1)S(1)} %bitcast.16, ...), custom_call_target="tpu_custom_call", output_to_operand_aliasing={{0}: (7, {})} | custom-call | flops 1200000000 | bytes 1800000 | tf_op jit(solution)/shard_map/conv/pallas_call | solution.py:237
  28.1 0.0 collective-permute-done.6.refs_1_
  28.1 0.9 %collective-permute-start.7 = (f32[144,128]{1,0:T(8,128)S(1)}, f32[144,128]{1,0:T(8,128)S(1)}, u32[]{:S(2)}, u32[]{:S(2)}) collective-permute-start(f32[144,128]{1,0:T(8,128)S(1)} %add_x.1.refs_6_.own), channel_id=1, source_target_pairs={{0,2},{1,3},{2,4},{3,5},{4,6},{5,7},{6,0},{7,1},{8,10},{9,11},{10,... | collective-permute-start | bytes 221192 | tf_op jit(solution)/shard_map/ppermute | solution.py:520
  29.0 2.4 %collective-permute-start.8 = (f32[144,128]{1,0:T(8,128)S(1)}, f32[144,128]{1,0:T(8,128)S(1)}, u32[]{:S(2)}, u32[]{:S(2)}) collective-permute-start(f32[144,128]{1,0:T(8,128)S(1)} %add_x.1.refs_6_.own), channel_id=1, source_target_pairs={{0,4},{1,5},{2,6},{3,7},{4,0},{5,1},{6,2},{7,3},{8,12},{9,13},{10,... | collective-permute-start | bytes 221192 | tf_op jit(solution)/shard_map/ppermute | solution.py:520
  31.4 0.4 collective-permute-start.9
  31.8 2.6 %conv.5 = (bf16[16,512,128]{2,1,0:T(8,128)(2,1)}, f32[8,128]{1,0:T(8,128)S(1)}) custom-call(bf16[1,512,128]{2,1,0:T(8,128)(2,1)S(1)} %collective-permute-done.near.refs_0_, bf16[1,512,128]{2,1,0:T(8,128)(2,1)S(1)} %collective-permute-done.1.far.refs_1_, bf16[16,512,128]{2,1,0:T(8,128)(2,1)S(1)} %bitcast.19, ...), custom_call_target="tpu_custom_call", output_to_operand_aliasing={{0}: (7, {})} | custom-call | flops 1800000000 | bytes 2700000 | tf_op jit(solution)/shard_map/conv/pallas_call | solution.py:237
  34.4 0.0 collective-permute-done.7.first
  34.4 0.0 collective-permute-done.8.second
  34.4 0.5 collective-permute-done.9.third
  34.9 4.0 %collective-permute-start.10 = (f32[576,128]{1,0:T(8,128)S(1)}, f32[576,128]{1,0:T(8,128)S(1)}, u32[]{:S(2)}, u32[]{:S(2)}) collective-permute-start(f32[576,128]{1,0:T(8,128)S(1)} %gather_y.1.refs_0_), channel_id=1, source_target_pairs={{0,1},{1,0},{2,3},{3,2},{4,5},{5,4},{6,7},{7,6},{8,9},{9,8},{10,11... | collective-permute-start | bytes 884744 | tf_op jit(solution)/shard_map/ppermute | solution.py:525
  39.7 0.5 collective-permute-done.10.refs_1_
  40.2 4.0 %image.1 = (bf16[16,64,128]{2,1,0:T(8,128)(2,1)S(1)}, f32[1,1]{1,0:T(1,128)}) custom-call(f32[576,128]{1,0:T(8,128)S(1)} %gather_y.1.refs_0_, f32[576,128]{1,0:T(8,128)S(1)} %collective-permute-done.10.refs_1_, f32[8,128]{1,0:T(8,128)S(1)} %get-tuple-element.33.rows.refs_2_, f32[1,512]{1,0:T(1,128)S(1)} %copy-done.4, bf16[8,9,128,128]{3,2,1,0:T(8,128)(2,1)S(1)} %copy-done.1, ...), custom_call_target="tpu_custom_call" | custom-call | flops 6000000000 | bytes 3528708 | tf_op jit(solution)/shard_map/image/pallas_call | solution.py:32
  44.2 20.0 %all_to_all.5.mine = bf16[16,64,128]{2,1,0:T(8,128)(2,1)S(1)} all-to-all(bf16[16,64,128]{2,1,0:T(8,128)(2,1)S(1)} %get-tuple-element.45), channel_id=1, replica_groups=mesh['samp'=16,'tok'=16] {'samp'}, dimensions={0} | all-to-all | bytes 524288 | tf_op jit(solution)/shard_map/all_to_all | solution.py:553
  64.2 1.9 %collective-permute-start.11 = (bf16[16,64,128]{2,1,0:T(8,128)(2,1)S(1)}, bf16[16,64,128]{2,1,0:T(8,128)(2,1)S(1)}, u32[]{:S(2)}, u32[]{:S(2)}) collective-permute-start(bf16[16,64,128]{2,1,0:T(8,128)(2,1)S(1)} %all_to_all.5.mine), channel_id=1, source_target_pairs={{0,1},{1,0},{2,3},{3,2},{4,5},{5,4},{6,7},{7,6},{8,9},{9,8},{10,11... | collective-permute-start | bytes 786440 | tf_op jit(solution)/shard_map/ppermute | solution.py:554
  66.1 1.2 %collective-permute-done.11.other = bf16[16,64,128]{2,1,0:T(8,128)(2,1)S(1)} collective-permute-done((bf16[16,64,128]{2,1,0:T(8,128)(2,1)S(1)}, bf16[16,64,128]{2,1,0:T(8,128)(2,1)S(1)}, u32[]{:S(2)}, u32[]{:S(2)}) %collective-permute-start.11) | collective-permute-done | bytes 262176 | tf_op jit(solution)/shard_map/ppermute | solution.py:554
  67.2 2.7 %final.1 = (f32[8,9,8,128]{3,2,1,0:T(8,128)}, f32[512,128]{1,0:T(8,128)}, f32[8,512]{1,0:T(8,128)}) custom-call(bf16[16,64,128]{2,1,0:T(8,128)(2,1)S(1)} %all_to_all.5.mine, bf16[16,64,128]{2,1,0:T(8,128)(2,1)S(1)} %collective-permute-done.11.other, f32[8,9,8,128]{3,2,1,0:T(8,128)S(1)} %dynamic-slice_convert_fusion.refs_8_.bank_s), custom_call_target="tpu_custom_call" | custom-call | bytes 819200 | tf_op jit(solution)/shard_map/final/pallas_call | solution.py:32
  (5 shorter events, 0.1 us)
Async XLA Ops:
  1.6 11.4 %collective-permute-start = (bf16[1,512,128]{2,1,0:T(8,128)(2,1)S(1)}, bf16[1,512,128]{2,1,0:T(8,128)(2,1)S(1)}, u32[]{:S(2)}, u32[]{:S(2)}) collective-permute-start(bf16[1,512,128]{2,1,0:T(8,128)(2,1)S(1)} %get-tuple-element.50), channel_id=1, source_target_pairs={{0,1},{1,0},{2,3},{3,2},{4,5},{5,4},{6,7},{7,6},{8,9},{9,8},{10,11... | collective-permute-start | bytes 393224 | tf_op jit(solution)/shard_map/ppermute | solution.py:458
  5.0 8.1 %collective-permute-start.1 = (bf16[1,512,128]{2,1,0:T(8,128)(2,1)S(1)}, bf16[1,512,128]{2,1,0:T(8,128)(2,1)S(1)}, u32[]{:S(2)}, u32[]{:S(2)}) collective-permute-start(bf16[1,512,128]{2,1,0:T(8,128)(2,1)S(1)} %get-tuple-element.49), channel_id=1, source_target_pairs={{1,2},{3,4},{5,6},{7,8},{9,10},{11,12},{13,14},{2,1},{4,3},{6,5},{... | collective-permute-start | bytes 393224 | tf_op jit(solution)/shard_map/ppermute | solution.py:457
  6.9 6.8 %copy-start.1 = (bf16[8,9,128,128]{3,2,1,0:T(8,128)(2,1)S(1)}, bf16[8,9,128,128]{3,2,1,0:T(8,128)(2,1)}, u32[]{:S(2)}) copy-start(bf16[8,9,128,128]{3,2,1,0:T(8,128)(2,1)} %refs_4_.1) | copy-start | bytes 7077892
  6.9 6.8 %copy-start.2 = (f32[512,128]{1,0:T(8,128)S(1)}, f32[512,128]{1,0:T(8,128)}, u32[]{:S(2)}) copy-start(f32[512,128]{1,0:T(8,128)} %refs_5_.1) | copy-start | bytes 786436
  6.9 6.8 %copy-start.3 = (f32[512,8]{0,1:T(8,128)S(1)}, f32[512,8]{0,1:T(8,128)}, u32[]{:S(2)}) copy-start(f32[512,8]{0,1:T(8,128)} %param.12) | copy-start | bytes 49156
  6.9 6.8 %copy-start.4 = (f32[1,512]{1,0:T(1,128)S(1)}, f32[1,512]{1,0:T(1,128)}, u32[]{:S(2)}) copy-start(f32[1,512]{1,0:T(1,128)} %refs_3_.1) | copy-start | bytes 6148
  13.6 1.7 %collective-permute-start.2 = (f32[576,128]{1,0:T(8,128)S(1)}, f32[576,128]{1,0:T(8,128)S(1)}, u32[]{:S(2)}, u32[]{:S(2)}) collective-permute-start(f32[576,128]{1,0:T(8,128)S(1)} %get-tuple-element.32), channel_id=1, source_target_pairs={{0,1},{1,0},{2,3},{3,2},{4,5},{5,4},{6,7},{7,6},{8,9},{9,8},{10,11... | collective-permute-start | bytes 884744 | tf_op jit(solution)/shard_map/ppermute | solution.py:506
  13.8 6.4 %copy-start = (bf16[1,16,512,128]{3,2,1,0:T(8,128)(2,1)S(1)}, bf16[1,16,512,128]{3,2,1,0:T(8,128)(2,1)}, u32[]{:S(2)}) copy-start(bf16[1,16,512,128]{3,2,1,0:T(8,128)(2,1)} %param.7) | copy-start | bytes 6291460
  15.3 7.4 %collective-permute-start.3 = (f32[144,128]{1,0:T(8,128)S(1)}, f32[144,128]{1,0:T(8,128)S(1)}, u32[]{:S(2)}, u32[]{:S(2)}) collective-permute-start(f32[144,128]{1,0:T(8,128)S(1)} %get-tuple-element.35), channel_id=1, source_target_pairs={{0,4},{1,5},{2,6},{3,7},{4,0},{5,1},{6,2},{7,3},{8,12},{9,13},{10,... | collective-permute-start | bytes 221192 | tf_op jit(solution)/shard_map/ppermute | solution.py:514
  17.5 5.3 %collective-permute-start.4 = (f32[144,128]{1,0:T(8,128)S(1)}, f32[144,128]{1,0:T(8,128)S(1)}, u32[]{:S(2)}, u32[]{:S(2)}) collective-permute-start(f32[144,128]{1,0:T(8,128)S(1)} %get-tuple-element.36), channel_id=1, source_target_pairs={{0,2},{1,3},{2,4},{3,5},{4,6},{5,7},{6,0},{7,1},{8,10},{9,11},{10,... | collective-permute-start | bytes 221192 | tf_op jit(solution)/shard_map/ppermute | solution.py:514
  19.3 3.6 %collective-permute-start.5 = (f32[144,128]{1,0:T(8,128)S(1)}, f32[144,128]{1,0:T(8,128)S(1)}, u32[]{:S(2)}, u32[]{:S(2)}) collective-permute-start(f32[144,128]{1,0:T(8,128)S(1)} %get-tuple-element.37), channel_id=1, source_target_pairs={{0,6},{1,7},{2,0},{3,1},{4,2},{5,3},{6,4},{7,5},{8,14},{9,15},{10,... | collective-permute-start | bytes 221192 | tf_op jit(solution)/shard_map/ppermute | solution.py:514
  22.9 5.2 %collective-permute-start.6 = (f32[144,128]{1,0:T(8,128)S(1)}, f32[144,128]{1,0:T(8,128)S(1)}, u32[]{:S(2)}, u32[]{:S(2)}) collective-permute-start(f32[144,128]{1,0:T(8,128)S(1)} %add_y.1.refs_6_.refs_0_), channel_id=1, source_target_pairs={{0,8},{1,9},{2,10},{3,11},{4,12},{5,13},{6,14},{7,15},{8,0},{9,1},... | collective-permute-start | bytes 221192 | tf_op jit(solution)/shard_map/ppermute | solution.py:517
  28.1 6.3 %collective-permute-start.7 = (f32[144,128]{1,0:T(8,128)S(1)}, f32[144,128]{1,0:T(8,128)S(1)}, u32[]{:S(2)}, u32[]{:S(2)}) collective-permute-start(f32[144,128]{1,0:T(8,128)S(1)} %add_x.1.refs_6_.own), channel_id=1, source_target_pairs={{0,2},{1,3},{2,4},{3,5},{4,6},{5,7},{6,0},{7,1},{8,10},{9,11},{10,... | collective-permute-start | bytes 221192 | tf_op jit(solution)/shard_map/ppermute | solution.py:520
  29.0 5.3 %collective-permute-start.8 = (f32[144,128]{1,0:T(8,128)S(1)}, f32[144,128]{1,0:T(8,128)S(1)}, u32[]{:S(2)}, u32[]{:S(2)}) collective-permute-start(f32[144,128]{1,0:T(8,128)S(1)} %add_x.1.refs_6_.own), channel_id=1, source_target_pairs={{0,4},{1,5},{2,6},{3,7},{4,0},{5,1},{6,2},{7,3},{8,12},{9,13},{10,... | collective-permute-start | bytes 221192 | tf_op jit(solution)/shard_map/ppermute | solution.py:520
  31.4 3.5 %collective-permute-start.9 = (f32[144,128]{1,0:T(8,128)S(1)}, f32[144,128]{1,0:T(8,128)S(1)}, u32[]{:S(2)}, u32[]{:S(2)}) collective-permute-start(f32[144,128]{1,0:T(8,128)S(1)} %add_x.1.refs_6_.own), channel_id=1, source_target_pairs={{0,6},{1,7},{2,0},{3,1},{4,2},{5,3},{6,4},{7,5},{8,14},{9,15},{10,... | collective-permute-start | bytes 221192 | tf_op jit(solution)/shard_map/ppermute | solution.py:520
  34.9 5.2 %collective-permute-start.10 = (f32[576,128]{1,0:T(8,128)S(1)}, f32[576,128]{1,0:T(8,128)S(1)}, u32[]{:S(2)}, u32[]{:S(2)}) collective-permute-start(f32[576,128]{1,0:T(8,128)S(1)} %gather_y.1.refs_0_), channel_id=1, source_target_pairs={{0,1},{1,0},{2,3},{3,2},{4,5},{5,4},{6,7},{7,6},{8,9},{9,8},{10,11... | collective-permute-start | bytes 884744 | tf_op jit(solution)/shard_map/ppermute | solution.py:525
  64.2 3.1 %collective-permute-start.11 = (bf16[16,64,128]{2,1,0:T(8,128)(2,1)S(1)}, bf16[16,64,128]{2,1,0:T(8,128)(2,1)S(1)}, u32[]{:S(2)}, u32[]{:S(2)}) collective-permute-start(bf16[16,64,128]{2,1,0:T(8,128)(2,1)S(1)} %all_to_all.5.mine), channel_id=1, source_target_pairs={{0,1},{1,0},{2,3},{3,2},{4,5},{5,4},{6,7},{7,6},{8,9},{9,8},{10,11... | collective-permute-start | bytes 786440 | tf_op jit(solution)/shard_map/ppermute | solution.py:554
